TPU v7x, 256 devices: a whole 4x4x8 slice. The times are simulated.
256 devices in a mesh: tile: 32 (over x, y, core), mem: 8 (over z).
Axes of the slice: x: 4, y: 4, z: 8, core: 2. Of those that a mesh axis runs over, the one named last changes fastest.
Arguments:
- members: bfloat16 [80, 4, 512, 512], P('mem', None, 'tile'), may hold values from -6 to 6
- weights: bfloat16 [65536, 128], P('tile'), may hold values from -0.5 to 0.5
- modes_in: float32 [4, 65536], P(None, 'tile'), may hold values from -120 to 120
- obs_tile: int32 [65536, 1], P('tile'), may hold values from 0 to 31; in each aligned block of 2048 rows (0 to 2047, 2048 to 4095, ...) at most 128 rows name the same one
- obs_block: int32 [65536], P('tile'), may hold values from 0 to 255
Outputs:
- modes_out: float32 [4, 65536], P(None, 'tile')
- eigen: float32 [4], replicated
Inputs may be any that keep to these rules, and one draw needn't show every extreme that they name: Among the observations of one tile, at most 128 name the same tile in obs_tile, a bound that some block reaches by one tile's observations.
All inputs are finite; a program needn't handle non-finite values.
Results may differ from a plain program's by a relative error of at most 0.0032.
Values may be sent and summed in bfloat16 or wider, within the bound.
No kernel may reach another device: no remote copies, remote signals or barrier semaphores. Data moves between devices by JAX's collectives and lax.ppermute only.
A program may use at most 128 MiB of HBM per device.

v0:
```python
import functools

import jax
import jax.numpy as jnp
from jax import lax
from jax.experimental import pallas as pl
from jax.experimental.pallas import tpu as pltpu
from jax.sharding import PartitionSpec as P

BX = 4
BY = 8
STEPS = 4
MODES = 4
ROWS = 80
TAIL = 64
HALO = 4
F32 = jnp.float32
BF16 = jnp.bfloat16


def stencil_points():
    counts = {(0, 0): 1}
    for _ in range(STEPS):
        wider = {}
        for (dx, dy), n in counts.items():
            for sx, sy in ((0, 0), (1, 0), (-1, 0), (0, 1), (0, -1)):
                key = (dx + sx, dy + sy)
                wider[key] = wider.get(key, 0) + n
        counts = wider
    return sorted((dx, dy, n) for (dx, dy), n in counts.items())


POINTS = stencil_points()
TOTAL = float(5**STEPS)

NT = (((1,), (1,)), ((), ()))
NN = (((1,), (0,)), ((), ()))


def matmul(a, b, dims):
    return lax.dot_general(a, b, dims, preferred_element_type=F32)


def iota(shape, dim):
    return lax.broadcasted_iota(jnp.int32, shape, dim)


def vmem(limit=40):
    return pltpu.CompilerParams(vmem_limit_bytes=limit << 20)


def pack_kernel(half_ref, w_ref, modes_ref, dest_ref, block_ref, out_ref, hot_ref, x_ref, tail_ref, xm_ref):
    n_tiles = out_ref.shape[0]
    obs = w_ref.shape[0]
    half = half_ref[0]
    q = iota((TAIL, 128), 0)
    source = (2 * half + (q >> 5)) * 32 + (q & 3) * 8 + ((q >> 2) & 7)
    order = jnp.where(iota((TAIL, 128), 1) == source, 1.0, 0.0).astype(BF16)
    x_ref[0:TAIL, :] = matmul(order, w_ref[...], NT).astype(BF16)
    m = modes_ref[...]
    hi = m.astype(BF16).astype(F32)
    mid = (m - hi).astype(BF16).astype(F32)
    lo = (m - hi) - mid
    tail_ref[0:4, :] = hi
    tail_ref[4:8, :] = mid
    tail_ref[8:12, :] = lo
    tail_ref[12:13, :] = (block_ref[...] + 1).astype(F32)
    tail_ref[13:16, :] = jnp.zeros((3, obs), F32)
    x_ref[TAIL:ROWS, :] = tail_ref[...].astype(BF16)
    chunk = 256
    upper = jnp.where(iota((chunk, chunk), 0) < iota((chunk, chunk), 1), 1.0, 0.0).astype(BF16)
    off = jnp.zeros((n_tiles, 1), F32)
    for c in range(obs // chunk):
        at = slice(c * chunk, (c + 1) * chunk)
        d = jnp.where(iota((n_tiles, chunk), 0) == dest_ref[:, at], 1.0, 0.0)
        before = matmul(d.astype(BF16), upper, NN) + off
        rank = jnp.sum(d * before, axis=0, keepdims=True).astype(jnp.int32)
        hot_ref[:, at] = jnp.where(iota((128, chunk), 0) == rank, 1.0, 0.0).astype(BF16)
        off = off + jnp.sum(d, axis=1, keepdims=True)
    group = 8
    for g in range(n_tiles // group):
        for t in range(group):
            here = jnp.where(dest_ref[...] == g * group + t, 1.0, 0.0)
            here = jnp.broadcast_to(here, (16, obs)).astype(BF16)
            for r in range(ROWS // 16):
                row = g * group * ROWS + t * ROWS + r * 16
                xm_ref[row : row + 16, :] = x_ref[r * 16 : r * 16 + 16, :] * here
        rows = group * ROWS
        sent = matmul(xm_ref[g * rows : (g + 1) * rows, :], hot_ref[...], NT)
        out_ref[g * group : (g + 1) * group] = sent.astype(BF16).reshape(group, ROWS, 128)


def extend(ext_ref, lead):
    lane = iota((ext_ref.shape[-2], 128), 1) & 63
    for n in range(HALO):
        low = pltpu.roll(ext_ref[lead, HALO + BY - HALO + n], 1, 1)
        ext_ref[lead, n] = jnp.where(lane == 0, ext_ref[lead, HALO + HALO - 1 - n], low)
        high = pltpu.roll(ext_ref[lead, HALO + n], 127, 1)
        ext_ref[lead, HALO + BY + n] = jnp.where(lane == 63, ext_ref[lead, HALO + BY - 1 - n], high)


def pair_kernel(scale, keep_ref, got_ref, low_ref, high_ref, out_ref, ext_ref):
    count = keep_ref.shape[0]
    total = 2 * count
    rows = keep_ref.shape[2]
    ny = keep_ref.shape[3]
    y = iota((ny, 128), 0)
    lane = iota((ny, 128), 1)
    for c in range(BY):
        low = jnp.where(y == (lane & 63) * BY + c, 1.0, 0.0)
        left = jnp.where(lane < 64, low, 0.0).astype(BF16)
        right = jnp.where(lane < 64, 0.0, low).astype(BF16)
        for part, ref in enumerate((keep_ref, got_ref)):
            r = matmul(ref[:, 0].reshape(count * rows, ny), left, NN) + matmul(
                ref[:, 1].reshape(count * rows, ny), right, NN
            )
            ext_ref[part * count : (part + 1) * count, HALO + c, HALO : HALO + rows, :] = r.reshape(
                count, rows, 128
            )
        for first, ref in ((0, low_ref), (HALO + rows, high_ref)):
            r = matmul(ref[0], left, NN) + matmul(ref[1], right, NN)
            for m in range(total):
                ext_ref[m, HALO + c, first : first + HALO, :] = r[m * HALO : (m + 1) * HALO, :]

    def widen(m, carry):
        extend(ext_ref, m)
        return carry

    lax.fori_loop(0, total, widen, 0)

    def plane(c, carry):
        for xv in range(rows // 8):

            def member(m, sums):
                here = ext_ref[m, HALO + c, HALO + xv * 8 : HALO + xv * 8 + 8, :]
                return tuple(
                    s + here * ext_ref[m, HALO + c + dy, HALO + xv * 8 + dx : HALO + xv * 8 + dx + 8, :]
                    for s, (dx, dy, n) in zip(sums, POINTS)
                )

            sums = lax.fori_loop(
                0, total, member, tuple(jnp.zeros((8, 128), F32) for _ in POINTS)
            )
            for i, (s, (dx, dy, n)) in enumerate(zip(sums, POINTS)):
                out_ref[i, c, xv * 8 : xv * 8 + 8, :] = s * (n * scale)
        return carry

    lax.fori_loop(0, BY, plane, 0)


def block_hot(tail):
    return jnp.where((iota((256, 128), 0) + 1).astype(F32) == tail[12:13, :], 1.0, 0.0).astype(BF16)


def spread_kernel(recv_ref, out_ref, low_ref, high_ref, g_ref, h_ref):
    n_tiles = recv_ref.shape[0]
    for s in range(n_tiles):
        at = slice(s * 128, (s + 1) * 128)
        w = recv_ref[s, 0:TAIL, :].astype(F32)
        tail = recv_ref[s, TAIL:ROWS, :].astype(F32)
        h_ref[:, at] = block_hot(tail)
        for l in range(2):
            for k in range(MODES):
                row = l * 128 + k * 32
                g_ref[row : row + 32, at] = (w[l * 32 : l * 32 + 32, :] * tail[k : k + 1, :]).astype(BF16)
    r = matmul(g_ref[...], h_ref[...], NT)
    for i in range(4):
        t = jnp.concatenate([r[0:128, i * 64 : i * 64 + 64], r[128:256, i * 64 : i * 64 + 64]], axis=1)
        if i == 0:
            low_ref[...] = t
        if i == 3:
            high_ref[...] = t
        for n in range(MODES * BY):
            out_ref[n, i * 4 : i * 4 + 4, :] = t[n * 4 : n * 4 + 4, :]


def image_kernel(recv_ref, f_ref, low_ref, high_ref, c_ref, out_ref, ext_ref, v_ref, t_ref, h_ref):
    n_tiles = recv_ref.shape[0]
    rows = f_ref.shape[1]
    for k in range(MODES):
        for c in range(BY):
            n = k * BY + c
            ext_ref[k, HALO + c, HALO : HALO + rows, :] = f_ref[n]
            ext_ref[k, HALO + c, 0:HALO, :] = low_ref[n * 4 : n * 4 + 4, :]
            ext_ref[k, HALO + c, HALO + rows : HALO + rows + HALO, :] = high_ref[n * 4 : n * 4 + 4, :]
        extend(ext_ref, k)

    def plane(c, carry):
        for xv in range(rows // 8):
            sums = [jnp.zeros((8, 128), F32) for _ in range(MODES)]
            for i, (dx, dy, n) in enumerate(POINTS):
                weight = c_ref[i, c, xv * 8 : xv * 8 + 8, :]
                first = HALO + xv * 8 + dx
                for k in range(MODES):
                    sums[k] = sums[k] + weight * ext_ref[k, HALO + c + dy, first : first + 8, :]
            for k in range(MODES):
                v_ref[k, c, xv * 8 : xv * 8 + 8, :] = sums[k]
        return carry

    lax.fori_loop(0, BY, plane, 0)
    for i in range(4):
        for k in range(MODES):
            for c in range(BY):
                n = k * BY + c
                t_ref[i, n * 4 : n * 4 + 4, :] = v_ref[k, c, i * 4 : i * 4 + 4, :]
    cov = jnp.concatenate(
        [
            jnp.concatenate([t_ref[i, :, l * 64 : l * 64 + 64] for i in range(4)], axis=1)
            for l in range(2)
        ],
        axis=0,
    )
    hi = cov.astype(BF16)
    lo = (cov - hi.astype(F32)).astype(BF16)
    both = jnp.concatenate([hi, lo], axis=0)
    for s in range(n_tiles):
        h_ref[:, s * 128 : (s + 1) * 128] = block_hot(recv_ref[s, TAIL:ROWS, :].astype(F32))
    group = 4
    cross = jnp.zeros((MODES, 128), F32)
    square = jnp.zeros((MODES, 128), F32)
    for g in range(n_tiles // group):
        picked = matmul(both, h_ref[:, g * group * 128 : (g + 1) * group * 128], NN)
        picked = picked[0:256] + picked[256:512]
        for j in range(group):
            s = g * group + j
            w = recv_ref[s, 0:TAIL, :].astype(F32)
            tail = recv_ref[s, TAIL:ROWS, :].astype(F32)
            first = (s % 2) * 4
            for k in range(MODES):
                part = picked[k * 32 : k * 32 + 32, j * 128 : (j + 1) * 128] * w[0:32]
                part = part + picked[128 + k * 32 : 160 + k * 32, j * 128 : (j + 1) * 128] * w[32:64]
                out_ref[0, s // 2, first + k : first + k + 1, :] = jnp.sum(part, axis=0, keepdims=True)
            mode = tail[0:4] + tail[4:8] + tail[8:12]
            cross = cross + mode * out_ref[0, s // 2, first : first + 4, :]
            square = square + mode * mode
    out_ref[0, n_tiles // 2, 0:4, :] = cross
    out_ref[0, n_tiles // 2, 4:8, :] = square * (1.0 / out_ref.shape[0])
    for m in range(1, out_ref.shape[0]):
        out_ref[m] = out_ref[0]


def gram_kernel(parts_ref, out_ref):
    n_tiles = out_ref.shape[0]
    groups = parts_ref.shape[0]
    pairs = n_tiles // 2
    sums = [jnp.zeros((8, 128), F32) for _ in range(MODES)]
    lane = iota((4, 128), 1)
    for p in range(pairs):
        z = parts_ref[0, p]
        for m in range(1, groups):
            z = z + parts_ref[m, p]
        out_ref[2 * p, 0:4, :] = z[0:4]
        out_ref[2 * p + 1, 0:4, :] = z[4:8]
        for d in range(MODES):
            sums[d] = sums[d] + z * (z if d == 0 else pltpu.roll(z, d, 0))
    last = parts_ref[0, pairs]
    for m in range(1, groups):
        last = last + parts_ref[m, pairs]
    stats = jnp.zeros((4, 128), F32)
    for d in range(MODES):
        both = sums[d][0:4] + sums[d][4:8]
        stats = jnp.where(lane == d, jnp.sum(both, axis=1, keepdims=True), stats)
    stats = jnp.where(lane == 4, jnp.sum(last[0:4], axis=1, keepdims=True), stats)
    stats = jnp.where(lane == 5, jnp.sum(last[4:8], axis=1, keepdims=True), stats)
    for s in range(n_tiles):
        out_ref[s, 4:8, :] = stats


def finish_kernel(back_ref, hot_ref, dest_ref, modes_ref, eigen_ref, split_ref):
    n_tiles = back_ref.shape[0]
    obs = dest_ref.shape[1]
    count = n_tiles * obs
    total = back_ref[0]
    for t in range(1, n_tiles):
        total = total + back_ref[t]

    def stat(k, lane):
        return total[4 + k : 5 + k, lane : lane + 1]

    def g(k, j):
        return stat(k, k - j) * (1.0 / count)

    low = {}
    for j in range(MODES):
        d = g(j, j)
        for p in range(j):
            d = d - low[j, p] * low[j, p]
        low[j, j] = jnp.sqrt(d)
        for k in range(j + 1, MODES):
            v = g(k, j)
            for p in range(j):
                v = v - low[k, p] * low[j, p]
            low[k, j] = v / low[j, j]
    a = back_ref[...].reshape(n_tiles * 8, 128)
    rows = n_tiles * 8
    hi = a.astype(BF16)
    rest = a - hi.astype(F32)
    mid = rest.astype(BF16)
    split_ref[0:rows, :] = hi
    split_ref[rows : 2 * rows, :] = mid
    split_ref[2 * rows : 3 * rows, :] = (rest - mid.astype(F32)).astype(BF16)
    chunk = 512
    for c in range(obs // chunk):
        at = slice(c * chunk, (c + 1) * chunk)
        r = matmul(split_ref[...], hot_ref[:, at], NN)
        r = (r[0:rows] + r[rows : 2 * rows]) + r[2 * rows : 3 * rows]
        dest = jnp.broadcast_to(dest_ref[:, at], (8, chunk))
        image = jnp.zeros((8, chunk), F32)
        for t in range(n_tiles):
            image = image + jnp.where(dest == t, r[t * 8 : t * 8 + 8], 0.0)
        done = []
        for k in range(MODES):
            v = image[k : k + 1]
            for p in range(k):
                v = v - low[k, p] * done[p]
            done.append(v / low[k, k])
            modes_ref[k : k + 1, at] = done[k]
    for k in range(MODES):
        eigen_ref[k : k + 1, :] = jnp.broadcast_to(stat(k, 4) / stat(k, 5), (1, 128))


VM = pl.BlockSpec(memory_space=pltpu.VMEM)
SM = pl.BlockSpec(memory_space=pltpu.SMEM)


def struct(shape, dtype):
    return jax.ShapeDtypeStruct(shape, dtype)


def on_device(members, weights, modes_in, obs_tile, obs_block):
    n_tiles = lax.axis_size("tile")
    n_groups = lax.axis_size("mem")
    obs, width = weights.shape
    count, levels, rows, ny = members.shape
    half = lax.axis_index("mem") % 2
    dest = obs_tile.reshape(1, obs)
    block = obs_block.reshape(1, obs)

    with jax.named_scope("pack"):
        sent, hot = pl.pallas_call(
            pack_kernel,
            in_specs=[SM, VM, VM, VM, VM],
            out_specs=[VM, VM],
            out_shape=[struct((n_tiles, ROWS, 128), BF16), struct((128, obs), BF16)],
            scratch_shapes=[
                pltpu.VMEM((ROWS, obs), BF16),
                pltpu.VMEM((16, obs), F32),
                pltpu.VMEM((n_tiles * ROWS, obs), BF16),
            ],
            compiler_params=vmem(),
        )(half.reshape(1), weights, modes_in, dest, block)
    with jax.named_scope("forward"):
        recv = lax.all_to_all(sent, "tile", 0, 0, tiled=True)

    with jax.named_scope("swap"):
        keep = lax.dynamic_slice_in_dim(members, 2 * half, 2, axis=1)
        give = lax.dynamic_slice_in_dim(members, 2 - 2 * half, 2, axis=1)
        got = lax.ppermute(give, "mem", [(m, m ^ 1) for m in range(n_groups)])
    up = [(t, (t + 1) % n_tiles) for t in range(n_tiles)]
    down = [(b, a) for a, b in up]

    def edge(first):
        both = jnp.concatenate([keep[:, :, first : first + HALO], got[:, :, first : first + HALO]], axis=0)
        return both.transpose(1, 0, 2, 3).reshape(2, 2 * count * HALO, ny)

    with jax.named_scope("member_edges"):
        m_low = lax.ppermute(edge(rows - HALO), "tile", up)
        m_high = lax.ppermute(edge(0), "tile", down)
    with jax.named_scope("pairs"):
        scale = 1.0 / (TOTAL * (count * n_groups - 1))
        pairs = pl.pallas_call(
            functools.partial(pair_kernel, scale),
            in_specs=[VM] * 4,
            out_specs=VM,
            out_shape=struct((len(POINTS), BY, rows, 128), F32),
            scratch_shapes=[pltpu.VMEM((2 * count, BY + 2 * HALO, rows + 2 * HALO, 128), F32)],
            compiler_params=vmem(),
        )(keep, got, m_low, m_high)

    with jax.named_scope("spread"):
        field, f_low, f_high = pl.pallas_call(
            spread_kernel,
            in_specs=[VM],
            out_specs=[VM] * 3,
            out_shape=[
                struct((MODES * BY, rows, 128), F32),
                struct((128, 128), F32),
                struct((128, 128), F32),
            ],
            scratch_shapes=[
                pltpu.VMEM((256, n_tiles * 128), BF16),
                pltpu.VMEM((256, n_tiles * 128), BF16),
            ],
            compiler_params=vmem(),
        )(recv)
    with jax.named_scope("spread_edges"):
        s_low = lax.ppermute(f_high, "tile", up)
        s_high = lax.ppermute(f_low, "tile", down)
    with jax.named_scope("images"):
        parts = pl.pallas_call(
            image_kernel,
            in_specs=[VM] * 5,
            out_specs=VM,
            out_shape=struct((n_groups, n_tiles // 2 + 1, 8, 128), F32),
            scratch_shapes=[
                pltpu.VMEM((MODES, BY + 2 * HALO, rows + 2 * HALO, 128), F32),
                pltpu.VMEM((MODES, BY, rows, 128), F32),
                pltpu.VMEM((4, 128, 128), F32),
                pltpu.VMEM((256, n_tiles * 128), BF16),
            ],
            compiler_params=vmem(),
        )(recv, field, s_low, s_high, pairs)
    with jax.named_scope("group_sum"):
        parts = lax.all_to_all(parts, "mem", 0, 0, tiled=True)
    with jax.named_scope("gram"):
        back = pl.pallas_call(
            gram_kernel,
            in_specs=[VM],
            out_specs=VM,
            out_shape=struct((n_tiles, 8, 128), F32),
        )(parts)
    with jax.named_scope("return"):
        back = lax.all_to_all(back, "tile", 0, 0, tiled=True)
    with jax.named_scope("finish"):
        modes_out, eigen = pl.pallas_call(
            finish_kernel,
            in_specs=[VM] * 3,
            out_specs=[VM] * 2,
            out_shape=[struct((MODES, obs), F32), struct((MODES, 128), F32)],
            scratch_shapes=[pltpu.VMEM((3 * n_tiles * 8, 128), BF16)],
            compiler_params=vmem(),
        )(back, hot, dest)
    return modes_out, eigen[:, 0]


def solution(mesh):
    in_specs = (
        P("mem", None, "tile", None),
        P("tile", None),
        P(None, "tile"),
        P("tile", None),
        P("tile"),
    )
    out_specs = (P(None, "tile"), P())
    return jax.shard_map(
        on_device, mesh=mesh, in_specs=in_specs, out_specs=out_specs, check_vma=False
    )
```

profile of v0, /device:TPU:1, one launch (start us, length us, event | category | flops | bytes accessed | tf_op | source)
XLA Modules:
  0.0 93.0 jit_solution(15188092785320827866)
XLA Ops:
  0.6 1.1 %constant_dynamic-slice_fusion.2 = (bf16[10,2,16,512]{3,2,1,0:T(8,128)(2,1)S(1)}, bf16[10,2,16,512]{3,2,1,0:T(8,128)(2,1)S(1)}) fusion(bf16[10,4,16,512]{3,2,1,0:T(8,128)(2,1)} %param.5, s32[]{:T(128)S(6)} %select_n.15, s32[]{:T(128)S(6)} %select_n.14), kind=kLoop, calls=%fused_computation.5 | loop fusion | bytes 1310728 | tf_op jit(solution)/shard_map/swap/dynamic_slice | solution.py:357
  1.8 2.6 %collective-permute-start.2 = (bf16[10,2,16,512]{3,2,1,0:T(8,128)(2,1)S(1)}, bf16[10,2,16,512]{3,2,1,0:T(8,128)(2,1)S(1)}, u32[]{:S(2)}, u32[]{:S(2)}) collective-permute-start(bf16[10,2,16,512]{3,2,1,0:T(8,128)(2,1)S(1)} %get-tuple-element.18), channel_id=1, source_target_pairs={{0,1},{1,0},{2,3},{3,2},{4,5},{5,4},{6,7},{7,6},{8,9},{9,8},{10,11... | collective-permute-start | bytes 983048 | tf_op jit(solution)/shard_map/swap/ppermute | solution.py:358
  4.3 0.0 copy-start
  4.3 1.0 %copy-done = bf16[2048,128]{1,0:T(8,128)(2,1)S(1)} copy-done((bf16[2048,128]{1,0:T(8,128)(2,1)S(1)}, bf16[2048,128]{1,0:T(8,128)(2,1)}, u32[]{:S(2)}) %copy-start) | copy-done | bytes 524312
  5.4 0.0 copy-start.1
  5.4 0.8 copy-done.1
  6.1 0.0 copy-start.2
  6.1 0.7 copy-done.2
  6.8 0.0 copy-start.4
  6.8 0.7 copy-done.4
  7.5 4.2 %pack.1 = (bf16[32,80,128]{2,1,0:T(8,128)(2,1)}, bf16[128,2048]{1,0:T(8,128)(2,1)S(1)}) custom-call(s32[1]{0:T(128)} %bitcast.half_ref, bf16[2048,128]{1,0:T(8,128)(2,1)S(1)} %copy-done, f32[4,2048]{1,0:T(4,128)S(1)} %copy-done.1, s32[1,2048]{1,0:T(1,128)S(1)} %bitcast.7, s32[1,2048]{1,0:T(1,128)S(1)} %bitcast.9), custom_call_target="tpu_custom_call" | custom-call | tf_op jit(solution)/shard_map/pack/pallas_call | solution.py:340
  11.7 8.1 %all-to-all-start = ((bf16[32,80,128]{2,1,0:T(8,128)(2,1)}), bf16[32,80,128]{2,1,0:T(8,128)(2,1)S(1)}, u32[]{:S(2)}, u32[]{:S(2)}) async-start(bf16[32,80,128]{2,1,0:T(8,128)(2,1)} %get-tuple-element.9), calls=%async_computation | async-start | bytes 1310720 | tf_op jit(solution)/shard_map/forward/all_to_all | solution.py:353
  19.8 1.1 %constant_dynamic-slice_fusion = (bf16[10,2,4,512]{3,2,1,0:T(4,128)(2,1)S(1)}, bf16[10,2,4,512]{3,2,1,0:T(4,128)(2,1)S(1)}) fusion(bf16[10,4,16,512]{3,2,1,0:T(8,128)(2,1)} %param.5, s32[]{:T(128)S(6)} %select_n.14, s32[]{:T(128)S(6)} %add.15), kind=kLoop, calls=%fused_computation.3 | loop fusion | bytes 327688 | tf_op jit(solution)/shard_map/member_edges/slice | solution.py:363
  20.9 0.0 collective-permute-done.2.got_ref
  20.9 0.1 fusion
  21.0 0.2 maximum_bitcast_fusion
  21.2 0.1 copy.9
  21.3 1.7 %collective-permute-start.3 = (bf16[2,80,512]{2,1,0:T(8,128)(2,1)S(1)}, bf16[2,80,512]{2,1,0:T(8,128)(2,1)S(1)}, u32[]{:S(2)}, u32[]{:S(2)}) collective-permute-start(bf16[2,80,512]{2,1,0:T(8,128)(2,1)S(1)} %reshape.22), channel_id=1, source_target_pairs={{0,8},{8,16},{16,24},{24,32},{32,40},{40,48},{48,56},{56,64},{64,7... | collective-permute-start | bytes 491528 | tf_op jit(solution)/shard_map/member_edges/ppermute | solution.py:367
  23.0 0.1 copy.10
  23.1 0.1 collective-permute-start.4
  23.2 9.9 %all-to-all-done.recv_ref = bf16[32,80,128]{2,1,0:T(8,128)(2,1)S(1)} async-done(((bf16[32,80,128]{2,1,0:T(8,128)(2,1)}), bf16[32,80,128]{2,1,0:T(8,128)(2,1)S(1)}, u32[]{:S(2)}, u32[]{:S(2)}) %all-to-all-start) | async-done | bytes 655392 | tf_op jit(solution)/shard_map/forward/all_to_all | solution.py:353
  33.1 1.6 %spread.1 = (f32[32,16,128]{2,1,0:T(8,128)S(1)}, f32[128,128]{1,0:T(8,128)S(1)}, f32[128,128]{1,0:T(8,128)S(1)}) custom-call(bf16[32,80,128]{2,1,0:T(8,128)(2,1)S(1)} %all-to-all-done.recv_ref), custom_call_target="tpu_custom_call" | custom-call | tf_op jit(solution)/shard_map/spread/pallas_call | solution.py:381
  34.6 0.1 collective-permute-start
  34.7 0.5 collective-permute-start.1
  35.2 0.0 collective-permute-done.3.low_ref
  35.2 0.0 collective-permute-done.4.high_ref
  35.2 11.6 %pairs.1.c_ref = f32[41,8,16,128]{3,2,1,0:T(8,128)S(1)} custom-call(bf16[10,2,16,512]{3,2,1,0:T(8,128)(2,1)S(1)} %get-tuple-element.19.keep_ref, bf16[10,2,16,512]{3,2,1,0:T(8,128)(2,1)S(1)} %collective-permute-done.2.got_ref, bf16[2,80,512]{2,1,0:T(8,128)(2,1)S(1)} %collective-permute-done.3.low_ref, bf16[2,80,512]{2,1,0:T(8,128)(2,1)S(1)} %collective-permute-done.4.high_ref), custom_call_target="tpu_custom_call" | custom-call | tf_op jit(solution)/shard_map/pairs/pallas_call | solution.py:371
  46.8 0.0 collective-permute-done.low_ref
  46.8 0.0 collective-permute-done.1.high_ref
  46.8 0.0 copy-start.3
  46.8 3.0 %images.1 = f32[8,17,8,128]{3,2,1,0:T(8,128)S(1)} custom-call(bf16[32,80,128]{2,1,0:T(8,128)(2,1)S(1)} %all-to-all-done.recv_ref, f32[32,16,128]{2,1,0:T(8,128)S(1)} %get-tuple-element.10.f_ref, f32[128,128]{1,0:T(8,128)S(1)} %collective-permute-done.low_ref, f32[128,128]{1,0:T(8,128)S(1)} %collective-permute-done.1.high_ref, f32[41,8,16,128]{3,2,1,0:T(8,128)S(1)} %pairs.1.c_ref), custom_call_target="tpu_custom_call" | custom-call | tf_op jit(solution)/shard_map/images/pallas_call | solution.py:400
  49.8 20.6 %all_to_all.15.parts_ref = f32[8,17,8,128]{3,2,1,0:T(8,128)} all-to-all(f32[8,17,8,128]{3,2,1,0:T(8,128)S(1)} %images.1), channel_id=1, replica_groups=mesh['tile'=32,'mem'=8] {'mem'}, dimensions={0} | all-to-all | bytes 1114112 | tf_op jit(solution)/shard_map/group_sum/all_to_all | solution.py:414
  70.3 1.8 %gram.1 = f32[32,8,128]{2,1,0:T(8,128)} custom-call(f32[8,17,8,128]{3,2,1,0:T(8,128)} %all_to_all.15.parts_ref), custom_call_target="tpu_custom_call" | custom-call | tf_op jit(solution)/shard_map/gram/pallas_call | solution.py:416
  72.2 18.6 %all_to_all.16.back_ref = f32[32,8,128]{2,1,0:T(8,128)S(1)} all-to-all(f32[32,8,128]{2,1,0:T(8,128)} %gram.1), channel_id=1, replica_groups=mesh['tile'=32,'mem'=8] {'tile'}, dimensions={0} | all-to-all | bytes 262144 | tf_op jit(solution)/shard_map/return/all_to_all | solution.py:423
  90.8 0.0 copy-done.3
  90.8 1.6 %finish.1 = (f32[4,2048]{1,0:T(4,128)}, f32[4,128]{1,0:T(4,128)S(1)}) custom-call(f32[32,8,128]{2,1,0:T(8,128)S(1)} %all_to_all.16.back_ref, bf16[128,2048]{1,0:T(8,128)(2,1)S(1)} %get-tuple-element.13.hot_ref, s32[1,2048]{1,0:T(1,128)S(1)} %bitcast.8), custom_call_target="tpu_custom_call" | custom-call | tf_op jit(solution)/shard_map/finish/pallas_call | solution.py:425
  92.4 0.6 slice_reduce_fusion
  (2 shorter events, 0.1 us)
Async XLA Ops:
  1.8 19.1 %collective-permute-start.2 = (bf16[10,2,16,512]{3,2,1,0:T(8,128)(2,1)S(1)}, bf16[10,2,16,512]{3,2,1,0:T(8,128)(2,1)S(1)}, u32[]{:S(2)}, u32[]{:S(2)}) collective-permute-start(bf16[10,2,16,512]{3,2,1,0:T(8,128)(2,1)S(1)} %get-tuple-element.18), channel_id=1, source_target_pairs={{0,1},{1,0},{2,3},{3,2},{4,5},{5,4},{6,7},{7,6},{8,9},{9,8},{10,11... | collective-permute-start | bytes 983048 | tf_op jit(solution)/shard_map/swap/ppermute | solution.py:358
  4.3 1.0 %copy-start = (bf16[2048,128]{1,0:T(8,128)(2,1)S(1)}, bf16[2048,128]{1,0:T(8,128)(2,1)}, u32[]{:S(2)}) copy-start(bf16[2048,128]{1,0:T(8,128)(2,1)} %w_ref.1) | copy-start | bytes 1572868
  5.4 0.8 copy-start.1
  6.1 0.7 copy-start.2
  6.8 0.7 copy-start.4
  11.7 21.3 %all-to-all-start = ((bf16[32,80,128]{2,1,0:T(8,128)(2,1)}), bf16[32,80,128]{2,1,0:T(8,128)(2,1)S(1)}, u32[]{:S(2)}, u32[]{:S(2)}) async-start(bf16[32,80,128]{2,1,0:T(8,128)(2,1)} %get-tuple-element.9), calls=%async_computation | async-start | bytes 1310720 | tf_op jit(solution)/shard_map/forward/all_to_all | solution.py:353
  21.3 13.9 %collective-permute-start.3 = (bf16[2,80,512]{2,1,0:T(8,128)(2,1)S(1)}, bf16[2,80,512]{2,1,0:T(8,128)(2,1)S(1)}, u32[]{:S(2)}, u32[]{:S(2)}) collective-permute-start(bf16[2,80,512]{2,1,0:T(8,128)(2,1)S(1)} %reshape.22), channel_id=1, source_target_pairs={{0,8},{8,16},{16,24},{24,32},{32,40},{40,48},{48,56},{56,64},{64,7... | collective-permute-start | bytes 491528 | tf_op jit(solution)/shard_map/member_edges/ppermute | solution.py:367
  23.1 12.1 %collective-permute-start.4 = (bf16[2,80,512]{2,1,0:T(8,128)(2,1)S(1)}, bf16[2,80,512]{2,1,0:T(8,128)(2,1)S(1)}, u32[]{:S(2)}, u32[]{:S(2)}) collective-permute-start(bf16[2,80,512]{2,1,0:T(8,128)(2,1)S(1)} %reshape.23), channel_id=1, source_target_pairs={{8,0},{16,8},{24,16},{32,24},{40,32},{48,40},{56,48},{64,56},{72,6... | collective-permute-start | bytes 491528 | tf_op jit(solution)/shard_map/member_edges/ppermute | solution.py:368
  34.6 12.2 %collective-permute-start = (f32[128,128]{1,0:T(8,128)S(1)}, f32[128,128]{1,0:T(8,128)S(1)}, u32[]{:S(2)}, u32[]{:S(2)}) collective-permute-start(f32[128,128]{1,0:T(8,128)S(1)} %get-tuple-element.11), channel_id=1, source_target_pairs={{0,8},{8,16},{16,24},{24,32},{32,40},{40,48},{48,56},{56,64},{64,7... | collective-permute-start | bytes 196616 | tf_op jit(solution)/shard_map/spread_edges/ppermute | solution.py:397
  34.7 12.1 %collective-permute-start.1 = (f32[128,128]{1,0:T(8,128)S(1)}, f32[128,128]{1,0:T(8,128)S(1)}, u32[]{:S(2)}, u32[]{:S(2)}) collective-permute-start(f32[128,128]{1,0:T(8,128)S(1)} %get-tuple-element.12), channel_id=1, source_target_pairs={{8,0},{16,8},{24,16},{32,24},{40,32},{48,40},{56,48},{64,56},{72,6... | collective-permute-start | bytes 196616 | tf_op jit(solution)/shard_map/spread_edges/ppermute | solution.py:398
  46.8 44.0 %copy-start.3 = (s32[2048,1]{0,1:T(1,128)S(1)}, s32[2048,1]{0,1:T(1,128)}, u32[]{:S(2)}) copy-start(s32[2048,1]{0,1:T(1,128)} %param.8) | copy-start | bytes 24580
where the time goes:
time: 93.6 us; the launch traced here: 93 us
  blocking collectives  39.2 us (42%)
  Pallas kernels  23.7 us (25%)
  starting transfers between devices  13 us (14%)
  waiting for transfers between devices  9.86 us (11%)
  local copies, waits for them, and re-layouts  6.3 us (7%)
    all_to_all x1, blocking collectives, on_device(): parts = lax.all_to_all(parts, 'mem', 0, 0, tiled=True)  20.6 us
    all_to_all x1, blocking collectives, on_device(): back = lax.all_to_all(back, 'tile', 0, 0, tiled=True)  18.6 us
    pallas_call x1, Pallas kernels, on_device(): pl.pallas_call(functools.partial(pair_kernel, scale), in_specs=[VM] * 4,...  11.6 us
    all_to_all x1, waiting for transfers between devices, on_device(): recv = lax.all_to_all(sent, 'tile', 0, 0, tiled=True)  9.85 us
    all_to_all x1, starting transfers between devices, on_device(): recv = lax.all_to_all(sent, 'tile', 0, 0, tiled=True)  8.05 us
    pallas_call x1, Pallas kernels, on_device(): pl.pallas_call(pack_kernel, in_specs=[SM, VM, VM, VM, VM], out_specs=[VM,...  4.19 us
    unnamed x10, local copies, waits for them, and re-layouts  3.2 us
    pallas_call x1, Pallas kernels, on_device(): pl.pallas_call(image_kernel, in_specs=[VM] * 5, out_specs=VM, out_shape=s...  2.95 us
  transfers between devices with their start and end apart: 6, of which 1 were waited for; matrix products, arithmetic and copies ran while one was open for 2% of the time, Pallas kernels for 19%

commit v1 on v0

v1 whole, which is shorter than its diff:
```python
import functools

import jax
import jax.numpy as jnp
from jax import lax
from jax.experimental import pallas as pl
from jax.experimental.pallas import tpu as pltpu
from jax.sharding import PartitionSpec as P

BX = 4
BY = 8
STEPS = 4
MODES = 4
ROWS = 80
TAIL = 64
HALO = 4
F32 = jnp.float32
BF16 = jnp.bfloat16


def stencil_points():
    counts = {(0, 0): 1}
    for _ in range(STEPS):
        wider = {}
        for (dx, dy), n in counts.items():
            for sx, sy in ((0, 0), (1, 0), (-1, 0), (0, 1), (0, -1)):
                key = (dx + sx, dy + sy)
                wider[key] = wider.get(key, 0) + n
        counts = wider
    return sorted((dx, dy, n) for (dx, dy), n in counts.items())


POINTS = [(dx, dy, n, i) for i, (dx, dy, n) in enumerate(stencil_points())]
EDGE_POINTS = [p for p in POINTS if p[0] > 0]
EDGE_POINTS = [(dx, dy, n, i) for i, (dx, dy, n, _) in enumerate(EDGE_POINTS)]
TOTAL = float(5**STEPS)

NT = (((1,), (1,)), ((), ()))
NN = (((1,), (0,)), ((), ()))


def matmul(a, b, dims):
    return lax.dot_general(a, b, dims, preferred_element_type=F32)


def iota(shape, dim):
    return lax.broadcasted_iota(jnp.int32, shape, dim)


def cost(us):
    return pl.CostEstimate(flops=0, bytes_accessed=us * 3_690_000, transcendentals=0)


def vmem(limit=16):
    return pltpu.CompilerParams(vmem_limit_bytes=limit << 20)


def pack_kernel(
    half_ref, w_any, modes_any, dest_any, block_any, members_any, out_ref, hot_ref, keep_ref,
    w_ref, modes_ref, dest_ref, block_ref, x_ref, tail_ref, xa_ref, xb_ref, sems,
):
    n_tiles = out_ref.shape[0]
    obs = w_ref.shape[0]
    half = half_ref[0]
    pairs = (
        (dest_any, dest_ref),
        (w_any, w_ref),
        (modes_any, modes_ref),
        (block_any, block_ref),
        (members_any.at[:, pl.ds(2 * half, 2)], keep_ref),
    )
    copies = [pltpu.make_async_copy(a, b, sems.at[i]) for i, (a, b) in enumerate(pairs)]
    for copy in copies:
        copy.start()
    copies[0].wait()
    chunk = 256
    upper = jnp.where(iota((chunk, chunk), 0) < iota((chunk, chunk), 1), 1.0, 0.0).astype(BF16)
    off = jnp.zeros((n_tiles, 1), F32)
    for c in range(obs // chunk):
        at = slice(c * chunk, (c + 1) * chunk)
        d = jnp.where(iota((n_tiles, chunk), 0) == dest_ref[:, at], 1.0, 0.0)
        before = matmul(d.astype(BF16), upper, NN) + off
        rank = jnp.sum(d * before, axis=0, keepdims=True).astype(jnp.int32)
        hot_ref[:, at] = jnp.where(iota((128, chunk), 0) == rank, 1.0, 0.0).astype(BF16)
        off = off + jnp.sum(d, axis=1, keepdims=True)
    for copy in copies[1:]:
        copy.wait()
    q = iota((TAIL, 128), 0)
    source = (2 * half + (q >> 5)) * 32 + (q & 3) * 8 + ((q >> 2) & 7)
    order = jnp.where(iota((TAIL, 128), 1) == source, 1.0, 0.0).astype(BF16)
    x_ref[0:TAIL, :] = matmul(order, w_ref[...], NT).astype(BF16)
    m = modes_ref[...]
    hi = m.astype(BF16).astype(F32)
    mid = (m - hi).astype(BF16).astype(F32)
    lo = (m - hi) - mid
    tail_ref[0:4, :] = hi
    tail_ref[4:8, :] = mid
    tail_ref[8:12, :] = lo
    tail_ref[12:13, :] = (block_ref[...] + 1).astype(F32)
    tail_ref[13:16, :] = jnp.zeros((3, obs), F32)
    x_ref[TAIL:ROWS, :] = tail_ref[...].astype(BF16)
    group = 8
    rows = group * ROWS

    def send(g, carry):
        for part, xm_ref in enumerate((xa_ref, xb_ref)):
            first = (2 * g + part) * group
            for t in range(group):
                here = jnp.where(dest_ref[...] == first + t, 1.0, 0.0)
                here = jnp.broadcast_to(here, (16, obs)).astype(BF16)
                for r in range(ROWS // 16):
                    row = t * ROWS + r * 16
                    xm_ref[row : row + 16, :] = x_ref[r * 16 : r * 16 + 16, :] * here
            sent = matmul(xm_ref[...], hot_ref[...], NT)
            out_ref[pl.ds(first, group)] = sent.astype(BF16).reshape(group, ROWS, 128)
        return carry

    lax.fori_loop(0, n_tiles // (2 * group), send, 0)


def extend(ext_ref, lead):
    lane = iota((ext_ref.shape[-2], 128), 1) & 63
    for n in range(HALO):
        low = pltpu.roll(ext_ref[lead, HALO + BY - HALO + n], 1, 1)
        ext_ref[lead, n] = jnp.where(lane == 0, ext_ref[lead, HALO + HALO - 1 - n], low)
        high = pltpu.roll(ext_ref[lead, HALO + n], 127, 1)
        ext_ref[lead, HALO + BY + n] = jnp.where(lane == 63, ext_ref[lead, HALO + BY - 1 - n], high)


def spread_rows(x, move):
    return matmul(x, move, NN)


def mover(ny):
    lane = iota((ny, ny), 1)
    return jnp.where(iota((ny, ny), 0) == (lane & 63) * BY + (lane >> 6), 1.0, 0.0).astype(BF16)


def join(first, second, p):
    a = first[:, p * 128 : (p + 1) * 128]
    b = second[:, p * 128 : (p + 1) * 128]
    left = iota(a.shape, 1) < 64
    return jnp.where(left, a, pltpu.roll(b, 64, 1)), jnp.where(left, pltpu.roll(a, 64, 1), b)


def pair_sums(center_of, ext_ref, out_ref, scale, c, at, points):
    total = ext_ref.shape[0]

    def member(m, sums):
        ext = {dy: ext_ref[m, HALO + c + dy, at : at + 8, :] for _, dy, _, _ in points}
        center = {dx: center_of(m, dx) for dx, _, _, _ in points}
        return tuple(s + center[dx] * ext[dy] for s, (dx, dy, _, _) in zip(sums, points))

    sums = lax.fori_loop(
        0, total, member, tuple(jnp.zeros((8, 128), F32) for _ in points), unroll=4
    )
    for s, (dx, dy, n, i) in zip(sums, points):
        out_ref[i, c, at : at + 8, :] = s * (n * scale)


def pair_kernel(scale, keep_ref, got_ref, out_ref, ends_ref, center_ref, ext_ref, y_ref):
    count = got_ref.shape[0]
    total = 2 * count
    rows = got_ref.shape[2]
    ny = got_ref.shape[3]
    move = mover(ny)
    side = count * 2 * rows
    y_ref[0:side, :] = spread_rows(keep_ref[...].reshape(side, ny), move)
    y_ref[side : 2 * side, :] = spread_rows(got_ref[...].reshape(side, ny), move)

    def place(m, carry):
        row = pl.multiple_of(m * 2 * rows, 2 * rows)
        first = y_ref[pl.ds(row, rows), :]
        second = y_ref[pl.ds(row + rows, rows), :]
        zero = jnp.zeros((8, 128), F32)
        for p in range(BY // 2):
            both = join(first, second, p)
            ends = [both[0][rows - HALO :], both[0][0:HALO], both[1][rows - HALO :], both[1][0:HALO]]
            ends_ref[m, p] = jnp.concatenate(ends, axis=0).astype(BF16)
            for i, v in enumerate(both):
                c = 2 * p + i
                ext_ref[m, HALO + c] = v
                center_ref[m, c, 0:8, :] = zero
                center_ref[m, c, 8 : 8 + rows, :] = v
                center_ref[m, c, 8 + rows : 16 + rows, :] = zero
        extend(ext_ref, m)
        return carry

    lax.fori_loop(0, total, place, 0, unroll=4)

    def plane(c, carry):
        for v in range(rows // 8):

            def center_of(m, dx):
                return center_ref[m, c, 8 + v * 8 - dx : 16 + v * 8 - dx, :]

            pair_sums(center_of, ext_ref, out_ref, scale, c, v * 8, POINTS)
        return carry

    lax.fori_loop(0, BY, plane, 0)


def pair_edge_kernel(scale, ends_ref, low_ref, high_ref, after_ref, out_ref, center_ref, ext_ref, y_ref):
    total = center_ref.shape[0]
    ny = low_ref.shape[2]
    side = 2 * total * HALO
    move = mover(ny)
    y_ref[0:side, :] = spread_rows(high_ref[...].reshape(side, ny), move)
    y_ref[side : 2 * side, :] = spread_rows(low_ref[...].reshape(side, ny), move)

    def place(m, carry):
        blocks = []
        for start in (0, side):
            row = pl.multiple_of(start + m * 2 * HALO, 8)
            blocks.append((y_ref[pl.ds(row, 8), :], y_ref[pl.ds(row + side // 2, 8), :]))
        top = iota((8, 128), 0) < HALO
        for p in range(BY // 2):
            for i, (high, low) in enumerate(zip(join(*blocks[0], p), join(*blocks[1], p))):
                ext_ref[2 * m, HALO + 2 * p + i] = jnp.where(top, high, pltpu.roll(low, HALO, 0))
                ext_ref[2 * m + 1, HALO + 2 * p + i] = jnp.where(top, pltpu.roll(high, HALO, 0), low)
        extend(ext_ref, 2 * m)
        extend(ext_ref, 2 * m + 1)
        for n in range(2):
            for p in range(BY // 2):
                ends = ends_ref[2 * m + n, p].astype(F32)
                for i in range(2):
                    center_ref[2 * m + n, 2 * p + i, 0:HALO, :] = ends[8 * i : 8 * i + HALO]
                    center_ref[2 * m + n, 2 * p + i, HALO : HALO + 8, :] = jnp.zeros((8, 128), F32)
                    center_ref[2 * m + n, 2 * p + i, HALO + 8 :, :] = ends[8 * i + HALO : 8 * i + 8]
        return carry

    lax.fori_loop(0, total // 2, place, 0, unroll=2)

    def plane(c, carry):
        def center_of(m, dx):
            return center_ref[m, c, HALO - dx : HALO + 8 - dx, :] + center_ref[m, c, HALO + dx : HALO + 8 + dx, :]

        pair_sums(center_of, ext_ref, out_ref, scale, c, 0, EDGE_POINTS)
        return carry

    lax.fori_loop(0, BY, plane, 0)


def block_hot(tail):
    return jnp.where((iota((256, 128), 0) + 1).astype(F32) == tail[12:13, :], 1.0, 0.0).astype(BF16)


def spread_kernel(recv_ref, after_ref, out_ref, low_ref, high_ref, g_ref, h_ref):
    n_tiles = recv_ref.shape[0]

    group = 8

    def sources(g, total):
        for j in range(group):
            at = slice(j * 128, (j + 1) * 128)
            w = recv_ref[g * group + j, 0:TAIL, :].astype(F32)
            tail = recv_ref[g * group + j, TAIL:ROWS, :].astype(F32)
            h_ref[:, at] = block_hot(tail)
            for l in range(2):
                for k in range(MODES):
                    row = l * 128 + k * 32
                    g_ref[row : row + 32, at] = (w[l * 32 : l * 32 + 32, :] * tail[k : k + 1, :]).astype(BF16)
        return total + matmul(g_ref[...], h_ref[...], NT)

    r = lax.fori_loop(0, n_tiles // group, sources, jnp.zeros((256, 256), F32))
    for i in range(4):
        t = jnp.concatenate([r[0:128, i * 64 : i * 64 + 64], r[128:256, i * 64 : i * 64 + 64]], axis=1)
        if i == 0:
            low_ref[...] = t
        if i == 3:
            high_ref[...] = t
        for n in range(MODES * BY):
            out_ref[n, i * 4 : i * 4 + 4, :] = t[n * 4 : n * 4 + 4, :]


def image_kernel(recv_ref, f_ref, low_ref, high_ref, c_ref, ce_ref, out_ref, ext_ref, side_ref, q_ref, t_ref):
    n_tiles = recv_ref.shape[0]
    rows = f_ref.shape[1]
    for k in range(MODES):
        for c in range(BY):
            n = k * BY + c
            ext_ref[k, HALO + c] = f_ref[n]
            side_ref[k, HALO + c, 0:HALO, :] = high_ref[n * 4 : n * 4 + 4, :]
            side_ref[k, HALO + c, HALO:8, :] = low_ref[n * 4 : n * 4 + 4, :]
        extend(ext_ref, k)
        extend(side_ref, k)

    def weigh(ref, v, c, points, weights):
        sums = [{} for _ in range(MODES)]
        for dx, dy, n, i in points:
            weight = weights[i, c, v * 8 : v * 8 + 8, :]
            for k in range(MODES):
                term = weight * ref[k, HALO + c + dy, v * 8 : v * 8 + 8, :]
                sums[k][dx] = sums[k][dx] + term if dx in sums[k] else term
        return sums

    def plane(cp, carry):
        for j in range(2):
            c = 2 * cp + j
            for v in range(rows // 8):
                for k, sums in enumerate(weigh(ext_ref, v, c, POINTS, c_ref)):
                    for dx, q in sums.items():
                        q_ref[k, j, dx + HALO, 8 + v * 8 : 16 + v * 8, :] = q
            for k, sums in enumerate(weigh(side_ref, 0, c, EDGE_POINTS, ce_ref)):
                for dx, q in sums.items():
                    q_ref[k, j, HALO - dx, 0:8, :] = q
                    q_ref[k, j, HALO + dx, rows + 8 : rows + 16, :] = q
        for k in range(MODES):
            for i in range(4):
                both = []
                for j in range(2):
                    at = 8 + i * 4
                    v = q_ref[k, j, HALO, at : at + 4, :]
                    for dx in range(-HALO, HALO + 1):
                        if dx != 0:
                            v = v + q_ref[k, j, dx + HALO, at + dx : at + dx + 4, :]
                    both.append(v)
                row = pl.multiple_of(k * 32 + cp * 8, 8)
                t_ref[i, pl.ds(row, 8), :] = jnp.concatenate(both, axis=0)
        return carry

    lax.fori_loop(0, BY // 2, plane, 0)
    cov = jnp.concatenate(
        [
            jnp.concatenate([t_ref[i, :, l * 64 : l * 64 + 64] for i in range(4)], axis=1)
            for l in range(2)
        ],
        axis=0,
    )
    hi = cov.astype(BF16)
    lo = (cov - hi.astype(F32)).astype(BF16)
    both = jnp.concatenate([hi, lo], axis=0)
    group = 8

    def image(g, carry):
        cross, square = carry
        hots = [block_hot(recv_ref[g * group + j, TAIL:ROWS, :].astype(F32)) for j in range(group)]
        picked = matmul(both, jnp.concatenate(hots, axis=1), NN)
        picked = picked[0:256] + picked[256:512]
        for j in range(group):
            s = g * group + j
            w = recv_ref[s, 0:TAIL, :].astype(F32)
            tail = recv_ref[s, TAIL:ROWS, :].astype(F32)
            first = (j % 2) * 4
            pair = g * (group // 2) + j // 2
            for k in range(MODES):
                part = picked[k * 32 : k * 32 + 32, j * 128 : (j + 1) * 128] * w[0:32]
                part = part + picked[128 + k * 32 : 160 + k * 32, j * 128 : (j + 1) * 128] * w[32:64]
                out_ref[pair, first + k : first + k + 1, :] = jnp.sum(part, axis=0, keepdims=True)
            mode = tail[0:4] + tail[4:8] + tail[8:12]
            cross = cross + mode * out_ref[pair, first : first + 4, :]
            square = square + mode * mode
        return cross, square

    zero = jnp.zeros((MODES, 128), F32)
    cross, square = lax.fori_loop(0, n_tiles // group, image, (zero, zero))
    out_ref[n_tiles // 2, 0:4, :] = cross
    out_ref[n_tiles // 2, 4:8, :] = square


def gram_kernel(groups, parts_ref, other_ref, out_ref):
    n_tiles = out_ref.shape[0]
    pairs = n_tiles // 2
    sums = [jnp.zeros((8, 128), F32) for _ in range(MODES)]
    lane = iota((4, 128), 1)
    for p in range(pairs):
        z = parts_ref[p] + other_ref[p]
        out_ref[2 * p, 0:4, :] = z[0:4]
        out_ref[2 * p + 1, 0:4, :] = z[4:8]
        for d in range(MODES):
            sums[d] = sums[d] + z * (z if d == 0 else pltpu.roll(z, d, 0))
    last = parts_ref[pairs] + other_ref[pairs]
    stats = jnp.zeros((4, 128), F32)
    for d in range(MODES):
        both = sums[d][0:4] + sums[d][4:8]
        stats = jnp.where(lane == d, jnp.sum(both, axis=1, keepdims=True), stats)
    stats = jnp.where(lane == 4, jnp.sum(last[0:4], axis=1, keepdims=True), stats)
    stats = jnp.where(lane == 5, jnp.sum(last[4:8], axis=1, keepdims=True) * (1.0 / groups), stats)
    for s in range(n_tiles):
        out_ref[s, 4:8, :] = stats


def finish_kernel(back_ref, hot_ref, dest_ref, modes_ref, eigen_ref, rows_ref, split_ref):
    n_tiles = back_ref.shape[0]
    obs = dest_ref.shape[1]
    count = n_tiles * obs
    total = back_ref[0]
    for t in range(1, n_tiles):
        total = total + back_ref[t]

    def stat(k, lane):
        return total[4 + k : 5 + k, lane : lane + 1]

    def g(k, j):
        return stat(k, k - j) * (1.0 / count)

    low = {}
    for j in range(MODES):
        d = g(j, j)
        for p in range(j):
            d = d - low[j, p] * low[j, p]
        low[j, j] = jnp.sqrt(d)
        for k in range(j + 1, MODES):
            v = g(k, j)
            for p in range(j):
                v = v - low[k, p] * low[j, p]
            low[k, j] = v / low[j, j]
    rows = n_tiles * MODES
    for t in range(n_tiles):
        rows_ref[t * MODES : (t + 1) * MODES, :] = back_ref[t, 0:MODES, :]
    a = rows_ref[...]
    hi = a.astype(BF16)
    rest = a - hi.astype(F32)
    mid = rest.astype(BF16)
    split_ref[0:rows, :] = hi
    split_ref[rows : 2 * rows, :] = mid
    split_ref[2 * rows : 3 * rows, :] = (rest - mid.astype(F32)).astype(BF16)
    chunk = 1024
    second = iota((8, chunk), 0) >> 2

    def finish(c, carry):
        at = pl.ds(pl.multiple_of(c * chunk, chunk), chunk)
        r = matmul(split_ref[...], hot_ref[:, at], NN)
        r = (r[0:rows] + r[rows : 2 * rows]) + r[2 * rows : 3 * rows]
        dest = jnp.broadcast_to(dest_ref[:, at], (8, chunk)) - second
        image = jnp.zeros((8, chunk), F32)
        for t in range(0, n_tiles, 2):
            image = image + jnp.where(dest == t, r[t * MODES : t * MODES + 8], 0.0)
        image = image[0:MODES] + image[MODES:8]
        done = []
        for k in range(MODES):
            v = image[k : k + 1]
            for p in range(k):
                v = v - low[k, p] * done[p]
            done.append(v / low[k, k])
            modes_ref[k : k + 1, at] = done[k]
        return carry

    lax.fori_loop(0, obs // chunk, finish, 0)
    eigen = jnp.zeros((1, 128), F32)
    for k in range(MODES):
        eigen = jnp.where(iota((1, 128), 1) == k, stat(k, 4) / stat(k, 5), eigen)
    eigen_ref[...] = eigen[0, 0:MODES]


VM = pl.BlockSpec(memory_space=pltpu.VMEM)
SM = pl.BlockSpec(memory_space=pltpu.SMEM)
ANY = pl.BlockSpec(memory_space=pl.ANY)
HBM = pl.BlockSpec(memory_space=pltpu.HBM)


def struct(shape, dtype):
    return jax.ShapeDtypeStruct(shape, dtype)


def on_device(members, weights, modes_in, obs_tile, obs_block):
    n_tiles = lax.axis_size("tile")
    n_groups = lax.axis_size("mem")
    obs, width = weights.shape
    count, levels, rows, ny = members.shape
    half = lax.axis_index("mem") % 2
    dest = obs_tile.reshape(1, obs)
    block = obs_block.reshape(1, obs)

    with jax.named_scope("swap"):
        give = lax.dynamic_slice_in_dim(members, 2 - 2 * half, 2, axis=1)
        got = lax.ppermute(give, "mem", [(m, m ^ 1) for m in range(n_groups)])
    with jax.named_scope("pack"):
        sent, hot, keep = pl.pallas_call(
            pack_kernel,
            in_specs=[SM] + [HBM] * 5,
            out_specs=[VM] * 3,
            out_shape=[
                struct((n_tiles, ROWS, 128), BF16),
                struct((128, obs), BF16),
                struct((count, 2, rows, ny), BF16),
            ],
            scratch_shapes=[
                pltpu.VMEM((obs, width), BF16),
                pltpu.VMEM((MODES, obs), F32),
                pltpu.VMEM((1, obs), jnp.int32),
                pltpu.VMEM((1, obs), jnp.int32),
                pltpu.VMEM((ROWS, obs), BF16),
                pltpu.VMEM((16, obs), F32),
                pltpu.VMEM((8 * ROWS, obs), BF16),
                pltpu.VMEM((8 * ROWS, obs), BF16),
                pltpu.SemaphoreType.DMA((5,)),
            ],
            compiler_params=vmem(60),
        )(half.reshape(1), weights, modes_in, dest, block, members)
    with jax.named_scope("forward"):
        recv = lax.all_to_all(sent, "tile", 0, 0, tiled=True)
    up = [(t, (t + 1) % n_tiles) for t in range(n_tiles)]
    down = [(b, a) for a, b in up]

    with jax.named_scope("member_edges"):
        def edge(first):
            both = jnp.concatenate([keep[:, :, first : first + HALO], got[:, :, first : first + HALO]], axis=0)
            return both.transpose(1, 0, 2, 3).reshape(2, 2 * count * HALO, ny)

        first, last = edge(0), edge(rows - HALO)
        m_low = lax.ppermute(last, "tile", up)
        m_high = lax.ppermute(first, "tile", down)
    scale = 1.0 / (TOTAL * (count * n_groups - 1))
    with jax.named_scope("pairs"):
        pairs, ends = pl.pallas_call(
            functools.partial(pair_kernel, scale),
            in_specs=[VM, VM],
            out_specs=[VM, VM],
            out_shape=[
                struct((len(POINTS), BY, rows, 128), F32),
                struct((2 * count, BY // 2, 16, 128), BF16),
            ],
            scratch_shapes=[
                pltpu.VMEM((2 * count, BY, rows + 16, 128), F32),
                pltpu.VMEM((2 * count, BY + 2 * HALO, rows, 128), F32),
                pltpu.VMEM((2 * count * 2 * rows, ny), F32),
            ],
            compiler_params=vmem(10),
            cost_estimate=cost(8),
        )(keep, got)

    with jax.named_scope("spread"):
        field, f_low, f_high = pl.pallas_call(
            spread_kernel,
            in_specs=[VM, ANY],
            out_specs=[VM] * 3,
            out_shape=[
                struct((MODES * BY, rows, 128), F32),
                struct((128, 128), F32),
                struct((128, 128), F32),
            ],
            scratch_shapes=[
                pltpu.VMEM((256, 8 * 128), BF16),
                pltpu.VMEM((256, 8 * 128), BF16),
            ],
            compiler_params=vmem(),
        )(recv, pairs)
    with jax.named_scope("spread_edges"):
        s_low = lax.ppermute(f_high, "tile", up)
        s_high = lax.ppermute(f_low, "tile", down)
    with jax.named_scope("pair_edges"):
        pairs_edge = pl.pallas_call(
            functools.partial(pair_edge_kernel, scale),
            in_specs=[VM, VM, VM, ANY],
            out_specs=VM,
            out_shape=struct((len(EDGE_POINTS), BY, 8, 128), F32),
            scratch_shapes=[
                pltpu.VMEM((2 * count, BY, 8 + 2 * HALO, 128), F32),
                pltpu.VMEM((2 * count, BY + 2 * HALO, 8, 128), F32),
                pltpu.VMEM((4 * 2 * count * HALO, ny), F32),
            ],
            compiler_params=vmem(6),
            cost_estimate=cost(3),
        )(ends, m_low, m_high, f_low)
    with jax.named_scope("images"):
        parts = pl.pallas_call(
            image_kernel,
            in_specs=[VM] * 6,
            out_specs=VM,
            out_shape=struct((n_tiles // 2 + 1, 8, 128), F32),
            scratch_shapes=[
                pltpu.VMEM((MODES, BY + 2 * HALO, rows, 128), F32),
                pltpu.VMEM((MODES, BY + 2 * HALO, 8, 128), F32),
                pltpu.VMEM((MODES, 2, 2 * HALO + 1, rows + 16, 128), F32),
                pltpu.VMEM((4, 128, 128), F32),
            ],
            compiler_params=vmem(),
        )(recv, field, s_low, s_high, pairs, pairs_edge)
    with jax.named_scope("group_sum"):
        for step in (1, 3):
            parts = parts + lax.ppermute(parts, "mem", [(m, m ^ step) for m in range(n_groups)])
        other = lax.ppermute(parts, "mem", [(m, n_groups - 1 - m) for m in range(n_groups)])
    with jax.named_scope("gram"):
        back = pl.pallas_call(
            functools.partial(gram_kernel, n_groups),
            in_specs=[VM, VM],
            out_specs=VM,
            out_shape=struct((n_tiles, 8, 128), F32),
            compiler_params=vmem(4),
        )(parts, other)
    with jax.named_scope("return"):
        back = lax.all_to_all(back, "tile", 0, 0, tiled=True)
    with jax.named_scope("finish"):
        modes_out, eigen = pl.pallas_call(
            finish_kernel,
            in_specs=[VM] * 3,
            out_specs=[VM] * 2,
            out_shape=[struct((MODES, obs), F32), struct((MODES,), F32)],
            scratch_shapes=[
                pltpu.VMEM((n_tiles * MODES, 128), F32),
                pltpu.VMEM((3 * n_tiles * MODES, 128), BF16),
            ],
            compiler_params=vmem(),
        )(back, hot, dest)
    return modes_out, eigen


def solution(mesh):
    in_specs = (
        P("mem", None, "tile", None),
        P("tile", None),
        P(None, "tile"),
        P("tile", None),
        P("tile"),
    )
    out_specs = (P(None, "tile"), P())
    return jax.shard_map(
        on_device, mesh=mesh, in_specs=in_specs, out_specs=out_specs, check_vma=False
    )
```

time: 93.6 us -> 80.8 us (0.86)
  blocking collectives: 39.2 us -> 18.6 us
  starting transfers between devices: 13 us -> 23.5 us
  waiting for transfers between devices: 9.86 us -> 7.64 us
    all_to_all x1 -> x0, blocking collectives: 20.6 us -> none  [on_device(): parts = lax.all_to_all(parts, 'mem', 0, 0, tiled=True)]
    all_to_all x1, waiting for transfers between devices: 9.85 us -> 0.01 us  [on_device(): recv = lax.all_to_all(sent, 'tile', 0, 0, tiled=True)]
    ppermute x2 -> x5, waiting for transfers between devices: 0.01 us -> 7.63 us  [the longest x2 5.5 us: on_device(): lax.ppermute(parts, 'mem', [(m, m ^ step) for m in range(n_groups)])]
    ppermute x2 -> x5, starting transfers between devices: 1.79 us -> 9.32 us  [the longest x1 4.65 us: on_device(): lax.ppermute(parts, 'mem', [(m, n_groups - 1 - m) for m in range(n_groups)])]
    ppermute x1, starting transfers between devices: 0.5 us -> 3.14 us  [on_device(): s_high = lax.ppermute(f_low, 'tile', down)]
    reshape x2, local copies, waits for them, and re-layouts: 0.09 us -> 1.4 us  [edge(): return both.transpose(1, 0, 2, 3).reshape(2, 2 * count * HALO, ny)]
    pallas_call x5 -> x6, Pallas kernels: 22.1 us -> 21.4 us  [the longest x1 6.97 us: on_device(): pl.pallas_call(functools.partial(pair_kernel, scale), in_specs=[VM, VM],...]
    unnamed x10 -> x14, local copies, waits for them, and re-layouts: 3.2 us -> 2.67 us
  transfers between devices with their start and end apart: 6 -> 9, of which waited for: 1 -> 3; matrix products, arithmetic and copies ran while one was open for 2% -> 4% of each run, Pallas kernels for 19% -> 22%
where the time goes in v1:
time: 80.8 us; the launch traced here: 80.4 us
  starting transfers between devices  23.5 us (29%)
  Pallas kernels  23.3 us (29%)
  blocking collectives  18.6 us (23%)
  waiting for transfers between devices  7.64 us (9%)
  local copies, waits for them, and re-layouts  6.33 us (8%)
  between operations  0.82 us (1%)
    all_to_all x1, blocking collectives, on_device(): back = lax.all_to_all(back, 'tile', 0, 0, tiled=True)  18.6 us
    all_to_all x1, starting transfers between devices, on_device(): recv = lax.all_to_all(sent, 'tile', 0, 0, tiled=True)  8.03 us
    pallas_call x1, Pallas kernels, on_device(): pl.pallas_call(functools.partial(pair_kernel, scale), in_specs=[VM, VM],...  6.97 us
    ppermute x2, waiting for transfers between devices, on_device(): lax.ppermute(parts, 'mem', [(m, m ^ step) for m in range(n_groups)])  5.5 us
    pallas_call x1, Pallas kernels, on_device(): pl.pallas_call(pack_kernel, in_specs=[SM] + [HBM] * 5, out_specs=[VM] * 3...  5.46 us
    ppermute x1, starting transfers between devices, on_device(): lax.ppermute(parts, 'mem', [(m, n_groups - 1 - m) for m in range(n_groups)])  4.65 us
    pallas_call x1, Pallas kernels, on_device(): pl.pallas_call(functools.partial(pair_edge_kernel, scale), in_specs=[VM,...  3.47 us
    pallas_call x1, Pallas kernels, on_device(): pl.pallas_call(image_kernel, in_specs=[VM] * 6, out_specs=VM, out_shape=s...  3.28 us
  transfers between devices with their start and end apart: 9, of which 3 were waited for; matrix products, arithmetic and copies ran while one was open for 4% of the time, Pallas kernels for 22%

profile of v1, /device:TPU:1, one launch (start us, length us, event | category | flops | bytes accessed | tf_op | source)
XLA Modules:
  0.0 80.4 jit_solution(7897317507243494903)
XLA Ops:
  0.6 1.0 %constant_dynamic-slice_fusion = bf16[10,2,16,512]{3,2,1,0:T(8,128)(2,1)S(1)} fusion(bf16[10,4,16,512]{3,2,1,0:T(8,128)(2,1)} %members_any.1, s32[]{:T(128)S(6)} %select_n.11), kind=kLoop, calls=%fused_computation.2 | loop fusion | bytes 655364 | tf_op jit(solution)/shard_map/swap/dynamic_slice | solution.py:466
  1.7 2.6 %collective-permute-start = (bf16[10,2,16,512]{3,2,1,0:T(8,128)(2,1)S(1)}, bf16[10,2,16,512]{3,2,1,0:T(8,128)(2,1)S(1)}, u32[]{:S(2)}, u32[]{:S(2)}) collective-permute-start(bf16[10,2,16,512]{3,2,1,0:T(8,128)(2,1)S(1)} %constant_dynamic-slice_fusion), channel_id=1, source_target_pairs={{0,1},{1,0},{2,3},{3,2},{4,5},{5,4},{6,7},{7,6},{8,9},{9,8},{10,11... | collective-permute-start | bytes 983048 | tf_op jit(solution)/shard_map/swap/ppermute | solution.py:467
  4.2 5.5 %pack.1 = (bf16[32,80,128]{2,1,0:T(8,128)(2,1)}, bf16[128,2048]{1,0:T(8,128)(2,1)}, bf16[10,2,16,512]{3,2,1,0:T(8,128)(2,1)}) custom-call(s32[1]{0:T(128)} %bitcast.half_ref, bf16[2048,128]{1,0:T(8,128)(2,1)} %w_any.1, f32[4,2048]{1,0:T(4,128)} %modes_any.1, s32[1,2048]{1,0:T(1,128)} %bitcast.7, s32[1,2048]{1,0:T(1,128)} %bitcast.9, ...), custom_call_target="tpu_custom_call" | custom-call | tf_op jit(solution)/shard_map/pack/pallas_call | solution.py:469
  9.7 8.0 %all-to-all-start = ((bf16[32,80,128]{2,1,0:T(8,128)(2,1)}), bf16[32,80,128]{2,1,0:T(8,128)(2,1)S(1)}, u32[]{:S(2)}, u32[]{:S(2)}) async-start(bf16[32,80,128]{2,1,0:T(8,128)(2,1)} %get-tuple-element.10), calls=%async_computation | async-start | bytes 1310720 | tf_op jit(solution)/shard_map/forward/all_to_all | solution.py:492
  17.7 1.1 %fusion = (bf16[10,2,4,512]{3,2,1,0:T(4,128)(2,1)S(1)}, bf16[10,2,4,512]{3,2,1,0:T(4,128)(2,1)S(1)}) fusion(bf16[10,2,16,512]{3,2,1,0:T(8,128)(2,1)} %get-tuple-element.11.keep_ref), kind=kLoop, calls=%fused_computation.3 | loop fusion | bytes 327680 | tf_op jit(solution)/shard_map/member_edges/slice | solution.py:498
  18.8 0.0 collective-permute-done.got_ref
  18.8 0.0 copy-start
  18.8 0.1 fusion.1
  18.9 0.2 maximum_bitcast_fusion
  19.1 0.1 copy.7
  19.2 0.7 reshape.22
  19.9 0.1 copy.8
  19.9 0.7 reshape.23
  20.6 0.2 collective-permute-start.4
  20.9 0.0 copy-done
  20.9 1.5 %collective-permute-start.3 = (bf16[2,80,512]{2,1,0:T(8,128)(2,1)}, bf16[2,80,512]{2,1,0:T(8,128)(2,1)}, u32[]{:S(2)}, u32[]{:S(2)}) collective-permute-start(bf16[2,80,512]{2,1,0:T(8,128)(2,1)} %reshape.22), channel_id=1, source_target_pairs={{0,8},{8,16},{16,24},{24,32},{32,40},{40,48},{48,56},{56,64},{64,7... | collective-permute-start | bytes 491528 | tf_op jit(solution)/shard_map/member_edges/ppermute | solution.py:502
  22.4 0.0 copy-start.1
  22.4 1.0 %copy-done.1 = bf16[10,2,16,512]{3,2,1,0:T(8,128)(2,1)S(1)} copy-done((bf16[10,2,16,512]{3,2,1,0:T(8,128)(2,1)S(1)}, bf16[10,2,16,512]{3,2,1,0:T(8,128)(2,1)}, u32[]{:S(2)}) %copy-start.1) | copy-done | bytes 327704
  23.4 0.0 copy-start.2
  23.4 1.0 %copy-done.2 = bf16[10,2,16,512]{3,2,1,0:T(8,128)(2,1)S(1)} copy-done((bf16[10,2,16,512]{3,2,1,0:T(8,128)(2,1)S(1)}, bf16[10,2,16,512]{3,2,1,0:T(8,128)(2,1)}, u32[]{:S(2)}) %copy-start.2) | copy-done | bytes 327704
  24.3 7.0 %pairs.1 = (f32[41,8,16,128]{3,2,1,0:T(8,128)S(1)}, bf16[20,4,16,128]{3,2,1,0:T(8,128)(2,1)S(1)}) custom-call(bf16[10,2,16,512]{3,2,1,0:T(8,128)(2,1)S(1)} %copy-done.2, bf16[10,2,16,512]{3,2,1,0:T(8,128)(2,1)S(1)} %copy-done.1), custom_call_target="tpu_custom_call" | custom-call | bytes 29520000 | tf_op jit(solution)/shard_map/pairs/pallas_call | solution.py:506
  31.3 0.0 copy-start.4
  31.3 0.7 copy-done.4
  32.0 0.0 all-to-all-done.recv_ref
  32.0 0.0 copy-start.5
  32.0 2.1 %spread.1 = (f32[32,16,128]{2,1,0:T(8,128)S(1)}, f32[128,128]{1,0:T(8,128)S(1)}, f32[128,128]{1,0:T(8,128)S(1)}) custom-call(bf16[32,80,128]{2,1,0:T(8,128)(2,1)S(1)} %all-to-all-done.recv_ref, f32[41,8,16,128]{3,2,1,0:T(8,128)S(1)} %get-tuple-element.12.after_ref.c_ref), custom_call_target="tpu_custom_call" | custom-call | tf_op jit(solution)/shard_map/spread/pallas_call | solution.py:524
  34.1 0.5 collective-permute-start.1
  34.6 3.1 %collective-permute-start.2 = (f32[128,128]{1,0:T(8,128)S(1)}, f32[128,128]{1,0:T(8,128)S(1)}, u32[]{:S(2)}, u32[]{:S(2)}) collective-permute-start(f32[128,128]{1,0:T(8,128)S(1)} %get-tuple-element.15.after_ref), channel_id=1, source_target_pairs={{8,0},{16,8},{24,16},{32,24},{40,32},{48,40},{56,48},{64,56},{72,6... | collective-permute-start | bytes 196616 | tf_op jit(solution)/shard_map/spread_edges/ppermute | solution.py:541
  37.8 0.0 collective-permute-done.4.high_ref
  37.8 0.0 collective-permute-done.3.low_ref
  37.8 0.0 copy-done.5
  37.8 3.5 %pair_edges.1.ce_ref = f32[16,8,8,128]{3,2,1,0:T(8,128)S(1)} custom-call(bf16[20,4,16,128]{3,2,1,0:T(8,128)(2,1)S(1)} %copy-done.5, bf16[2,80,512]{2,1,0:T(8,128)(2,1)} %collective-permute-done.3.low_ref, bf16[2,80,512]{2,1,0:T(8,128)(2,1)S(1)} %collective-permute-done.4.high_ref, f32[128,128]{1,0:T(8,128)S(1)} %get-tuple-element.15.after_ref), custom_call_target="tpu_custom_call" | custom-call | bytes 11070000 | tf_op jit(solution)/shard_map/pair_edges/pallas_call | solution.py:543
  41.3 0.0 copy-start.3
  41.3 0.0 copy-start.6
  41.3 0.0 collective-permute-done.1.low_ref
  41.3 0.0 collective-permute-done.2.high_ref
  41.3 3.3 %images.1 = f32[17,8,128]{2,1,0:T(8,128)S(1)} custom-call(bf16[32,80,128]{2,1,0:T(8,128)(2,1)S(1)} %all-to-all-done.recv_ref, f32[32,16,128]{2,1,0:T(8,128)S(1)} %get-tuple-element.13.f_ref, f32[128,128]{1,0:T(8,128)S(1)} %collective-permute-done.1.low_ref, f32[128,128]{1,0:T(8,128)S(1)} %collective-permute-done.2.high_ref, ...), custom_call_target="tpu_custom_call" | custom-call | tf_op jit(solution)/shard_map/images/pallas_call | solution.py:557
  44.6 0.1 collective-permute-start.5
  44.7 3.1 %collective-permute-done.5 = f32[17,8,128]{2,1,0:T(8,128)S(1)} collective-permute-done((f32[17,8,128]{2,1,0:T(8,128)S(1)}, f32[17,8,128]{2,1,0:T(8,128)S(1)}, u32[]{:S(2)}, u32[]{:S(2)}) %collective-permute-start.5) | collective-permute-done | bytes 69664 | tf_op jit(solution)/shard_map/group_sum/ppermute | solution.py:572
  47.8 2.8 %collective-permute-start.6 = (f32[17,8,128]{2,1,0:T(8,128)S(1)}, f32[17,8,128]{2,1,0:T(8,128)S(1)}, u32[]{:S(2)}, u32[]{:S(2)}) collective-permute-start(f32[17,8,128]{2,1,0:T(8,128)S(1)} %add.16), channel_id=1, source_target_pairs={{0,3},{1,2},{2,1},{3,0},{4,7},{5,6},{6,5},{7,4},{8,11},{9,10},{10,... | collective-permute-start | bytes 208904 | tf_op jit(solution)/shard_map/group_sum/ppermute | solution.py:572
  50.7 2.4 %collective-permute-done.6 = f32[17,8,128]{2,1,0:T(8,128)S(1)} collective-permute-done((f32[17,8,128]{2,1,0:T(8,128)S(1)}, f32[17,8,128]{2,1,0:T(8,128)S(1)}, u32[]{:S(2)}, u32[]{:S(2)}) %collective-permute-start.6) | collective-permute-done | bytes 69664 | tf_op jit(solution)/shard_map/group_sum/ppermute | solution.py:572
  53.0 4.7 %collective-permute-start.7 = (f32[17,8,128]{2,1,0:T(8,128)S(1)}, f32[17,8,128]{2,1,0:T(8,128)S(1)}, u32[]{:S(2)}, u32[]{:S(2)}) collective-permute-start(f32[17,8,128]{2,1,0:T(8,128)S(1)} %add.17.parts_ref), channel_id=1, source_target_pairs={{0,7},{1,6},{2,5},{3,4},{4,3},{5,2},{6,1},{7,0},{8,15},{9,14},{10,... | collective-permute-start | bytes 208904 | tf_op jit(solution)/shard_map/group_sum/ppermute | solution.py:573
  57.7 2.1 %collective-permute-done.7.other_ref = f32[17,8,128]{2,1,0:T(8,128)S(1)} collective-permute-done((f32[17,8,128]{2,1,0:T(8,128)S(1)}, f32[17,8,128]{2,1,0:T(8,128)S(1)}, u32[]{:S(2)}, u32[]{:S(2)}) %collective-permute-start.7) | collective-permute-done | bytes 69664 | tf_op jit(solution)/shard_map/group_sum/ppermute | solution.py:573
  59.8 0.1 gram.1
  59.9 18.6 %all_to_all.10.back_ref = f32[32,8,128]{2,1,0:T(8,128)S(1)} all-to-all(f32[32,8,128]{2,1,0:T(8,128)S(1)} %gram.1), channel_id=1, replica_groups=mesh['tile'=32,'mem'=8] {'tile'}, dimensions={0} | all-to-all | bytes 262144 | tf_op jit(solution)/shard_map/return/all_to_all | solution.py:583
  78.5 0.0 copy-done.3
  78.5 0.0 copy-done.6
  78.5 1.9 %finish.1 = (f32[4,2048]{1,0:T(4,128)}, f32[4]{0:T(128)}) custom-call(f32[32,8,128]{2,1,0:T(8,128)S(1)} %all_to_all.10.back_ref, bf16[128,2048]{1,0:T(8,128)(2,1)S(1)} %copy-done.3, s32[1,2048]{1,0:T(1,128)S(1)} %bitcast.8), custom_call_target="tpu_custom_call" | custom-call | tf_op jit(solution)/shard_map/finish/pallas_call | solution.py:585
  (2 shorter events, 0.0 us)
Async XLA Ops:
  1.7 17.1 %collective-permute-start = (bf16[10,2,16,512]{3,2,1,0:T(8,128)(2,1)S(1)}, bf16[10,2,16,512]{3,2,1,0:T(8,128)(2,1)S(1)}, u32[]{:S(2)}, u32[]{:S(2)}) collective-permute-start(bf16[10,2,16,512]{3,2,1,0:T(8,128)(2,1)S(1)} %constant_dynamic-slice_fusion), channel_id=1, source_target_pairs={{0,1},{1,0},{2,3},{3,2},{4,5},{5,4},{6,7},{7,6},{8,9},{9,8},{10,11... | collective-permute-start | bytes 983048 | tf_op jit(solution)/shard_map/swap/ppermute | solution.py:467
  9.7 22.4 %all-to-all-start = ((bf16[32,80,128]{2,1,0:T(8,128)(2,1)}), bf16[32,80,128]{2,1,0:T(8,128)(2,1)S(1)}, u32[]{:S(2)}, u32[]{:S(2)}) async-start(bf16[32,80,128]{2,1,0:T(8,128)(2,1)} %get-tuple-element.10), calls=%async_computation | async-start | bytes 1310720 | tf_op jit(solution)/shard_map/forward/all_to_all | solution.py:492
  18.8 2.1 %copy-start = (bf16[10,2,16,512]{3,2,1,0:T(8,128)(2,1)}, bf16[10,2,16,512]{3,2,1,0:T(8,128)(2,1)S(1)}, u32[]{:S(2)}) copy-start(bf16[10,2,16,512]{3,2,1,0:T(8,128)(2,1)S(1)} %collective-permute-done.got_ref) | copy-start | bytes 983044
  20.6 17.1 %collective-permute-start.4 = (bf16[2,80,512]{2,1,0:T(8,128)(2,1)}, bf16[2,80,512]{2,1,0:T(8,128)(2,1)S(1)}, u32[]{:S(2)}, u32[]{:S(2)}) collective-permute-start(bf16[2,80,512]{2,1,0:T(8,128)(2,1)} %reshape.23), channel_id=1, source_target_pairs={{8,0},{16,8},{24,16},{32,24},{40,32},{48,40},{56,48},{64,56},{72,6... | collective-permute-start | bytes 491528 | tf_op jit(solution)/shard_map/member_edges/ppermute | solution.py:503
  20.9 16.9 %collective-permute-start.3 = (bf16[2,80,512]{2,1,0:T(8,128)(2,1)}, bf16[2,80,512]{2,1,0:T(8,128)(2,1)}, u32[]{:S(2)}, u32[]{:S(2)}) collective-permute-start(bf16[2,80,512]{2,1,0:T(8,128)(2,1)} %reshape.22), channel_id=1, source_target_pairs={{0,8},{8,16},{16,24},{24,32},{32,40},{40,48},{48,56},{56,64},{64,7... | collective-permute-start | bytes 491528 | tf_op jit(solution)/shard_map/member_edges/ppermute | solution.py:502
  22.4 1.0 %copy-start.1 = (bf16[10,2,16,512]{3,2,1,0:T(8,128)(2,1)S(1)}, bf16[10,2,16,512]{3,2,1,0:T(8,128)(2,1)}, u32[]{:S(2)}) copy-start(bf16[10,2,16,512]{3,2,1,0:T(8,128)(2,1)} %copy-done) | copy-start | bytes 983044
  23.4 1.0 %copy-start.2 = (bf16[10,2,16,512]{3,2,1,0:T(8,128)(2,1)S(1)}, bf16[10,2,16,512]{3,2,1,0:T(8,128)(2,1)}, u32[]{:S(2)}) copy-start(bf16[10,2,16,512]{3,2,1,0:T(8,128)(2,1)} %get-tuple-element.11.keep_ref) | copy-start | bytes 983044
  31.3 0.7 copy-start.4
  32.0 5.7 %copy-start.5 = (bf16[20,4,16,128]{3,2,1,0:T(8,128)(2,1)S(1)}, bf16[20,4,16,128]{3,2,1,0:T(8,128)(2,1)}, u32[]{:S(2)}) copy-start(bf16[20,4,16,128]{3,2,1,0:T(8,128)(2,1)} %copy-done.4) | copy-start | bytes 983044
  34.1 7.1 %collective-permute-start.1 = (f32[128,128]{1,0:T(8,128)S(1)}, f32[128,128]{1,0:T(8,128)S(1)}, u32[]{:S(2)}, u32[]{:S(2)}) collective-permute-start(f32[128,128]{1,0:T(8,128)S(1)} %get-tuple-element.14), channel_id=1, source_target_pairs={{0,8},{8,16},{16,24},{24,32},{32,40},{40,48},{48,56},{56,64},{64,7... | collective-permute-start | bytes 196616 | tf_op jit(solution)/shard_map/spread_edges/ppermute | solution.py:540
  34.6 6.7 %collective-permute-start.2 = (f32[128,128]{1,0:T(8,128)S(1)}, f32[128,128]{1,0:T(8,128)S(1)}, u32[]{:S(2)}, u32[]{:S(2)}) collective-permute-start(f32[128,128]{1,0:T(8,128)S(1)} %get-tuple-element.15.after_ref), channel_id=1, source_target_pairs={{8,0},{16,8},{24,16},{32,24},{40,32},{48,40},{56,48},{64,56},{72,6... | collective-permute-start | bytes 196616 | tf_op jit(solution)/shard_map/spread_edges/ppermute | solution.py:541
  41.3 37.3 %copy-start.3 = (bf16[128,2048]{1,0:T(8,128)(2,1)S(1)}, bf16[128,2048]{1,0:T(8,128)(2,1)}, u32[]{:S(2)}) copy-start(bf16[128,2048]{1,0:T(8,128)(2,1)} %get-tuple-element.17.hot_ref) | copy-start | bytes 1572868
  41.3 37.3 %copy-start.6 = (s32[2048,1]{0,1:T(1,128)S(1)}, s32[2048,1]{0,1:T(1,128)}, u32[]{:S(2)}) copy-start(s32[2048,1]{0,1:T(1,128)} %param.8) | copy-start | bytes 24580
  44.6 3.2 %collective-permute-start.5 = (f32[17,8,128]{2,1,0:T(8,128)S(1)}, f32[17,8,128]{2,1,0:T(8,128)S(1)}, u32[]{:S(2)}, u32[]{:S(2)}) collective-permute-start(f32[17,8,128]{2,1,0:T(8,128)S(1)} %images.1), channel_id=1, source_target_pairs={{0,1},{1,0},{2,3},{3,2},{4,5},{5,4},{6,7},{7,6},{8,9},{9,8},{10,11... | collective-permute-start | bytes 208904 | tf_op jit(solution)/shard_map/group_sum/ppermute | solution.py:572
  47.8 5.2 %collective-permute-start.6 = (f32[17,8,128]{2,1,0:T(8,128)S(1)}, f32[17,8,128]{2,1,0:T(8,128)S(1)}, u32[]{:S(2)}, u32[]{:S(2)}) collective-permute-start(f32[17,8,128]{2,1,0:T(8,128)S(1)} %add.16), channel_id=1, source_target_pairs={{0,3},{1,2},{2,1},{3,0},{4,7},{5,6},{6,5},{7,4},{8,11},{9,10},{10,... | collective-permute-start | bytes 208904 | tf_op jit(solution)/shard_map/group_sum/ppermute | solution.py:572
  53.0 6.8 %collective-permute-start.7 = (f32[17,8,128]{2,1,0:T(8,128)S(1)}, f32[17,8,128]{2,1,0:T(8,128)S(1)}, u32[]{:S(2)}, u32[]{:S(2)}) collective-permute-start(f32[17,8,128]{2,1,0:T(8,128)S(1)} %add.17.parts_ref), channel_id=1, source_target_pairs={{0,7},{1,6},{2,5},{3,4},{4,3},{5,2},{6,1},{7,0},{8,15},{9,14},{10,... | collective-permute-start | bytes 208904 | tf_op jit(solution)/shard_map/group_sum/ppermute | solution.py:573

commit v2 on v1

--- a/solution.py
+++ b/solution.py
@@ -34,6 +34,8 @@
 EDGE_POINTS = [p for p in POINTS if p[0] > 0]
 EDGE_POINTS = [(dx, dy, n, i) for i, (dx, dy, n, _) in enumerate(EDGE_POINTS)]
 TOTAL = float(5**STEPS)
+
+PAIRS_KIB = 65536 - 12000
 
 NT = (((1,), (1,)), ((), ()))
 NN = (((1,), (0,)), ((), ()))
@@ -158,15 +160,17 @@
         out_ref[i, c, at : at + 8, :] = s * (n * scale)
 
 
-def pair_kernel(scale, keep_ref, got_ref, out_ref, ends_ref, center_ref, ext_ref, y_ref):
+def pair_kernel(
+    scale, keep_ref, got_ref, out_any, ends_ref, out_ref, center_ref, ext_ref, y_ref, sem
+):
     count = got_ref.shape[0]
     total = 2 * count
     rows = got_ref.shape[2]
     ny = got_ref.shape[3]
     move = mover(ny)
     side = count * 2 * rows
-    y_ref[0:side, :] = spread_rows(keep_ref[...].reshape(side, ny), move)
-    y_ref[side : 2 * side, :] = spread_rows(got_ref[...].reshape(side, ny), move)
+    for i, ref in enumerate((keep_ref, got_ref)):
+        y_ref[i * side : (i + 1) * side, :] = spread_rows(ref[...].reshape(side, ny), move)
 
     def place(m, carry):
         row = pl.multiple_of(m * 2 * rows, 2 * rows)
@@ -195,18 +199,21 @@
                 return center_ref[m, c, 8 + v * 8 - dx : 16 + v * 8 - dx, :]
 
             pair_sums(center_of, ext_ref, out_ref, scale, c, v * 8, POINTS)
+        pltpu.make_async_copy(out_ref.at[:, c], out_any.at[:, c], sem).start()
         return carry
 
     lax.fori_loop(0, BY, plane, 0)
+    pltpu.make_async_copy(out_ref, out_any, sem).wait()
 
 
 def pair_edge_kernel(scale, ends_ref, low_ref, high_ref, after_ref, out_ref, center_ref, ext_ref, y_ref):
     total = center_ref.shape[0]
-    ny = low_ref.shape[2]
+    ny = low_ref.shape[3]
     side = 2 * total * HALO
     move = mover(ny)
-    y_ref[0:side, :] = spread_rows(high_ref[...].reshape(side, ny), move)
-    y_ref[side : 2 * side, :] = spread_rows(low_ref[...].reshape(side, ny), move)
+    for start, ref in ((0, high_ref), (side, low_ref)):
+        rows = [ref[m, l].astype(F32) for l in range(2) for m in range(total)]
+        y_ref[start : start + side, :] = spread_rows(jnp.concatenate(rows, axis=0).astype(BF16), move)
 
     def place(m, carry):
         blocks = []
@@ -436,7 +443,7 @@
             modes_ref[k : k + 1, at] = done[k]
         return carry
 
-    lax.fori_loop(0, obs // chunk, finish, 0)
+    lax.fori_loop(0, obs // chunk, finish, 0, unroll=True)
     eigen = jnp.zeros((1, 128), F32)
     for k in range(MODES):
         eigen = jnp.where(iota((1, 128), 1) == k, stat(k, 4) / stat(k, 5), eigen)
@@ -495,8 +502,7 @@
 
     with jax.named_scope("member_edges"):
         def edge(first):
-            both = jnp.concatenate([keep[:, :, first : first + HALO], got[:, :, first : first + HALO]], axis=0)
-            return both.transpose(1, 0, 2, 3).reshape(2, 2 * count * HALO, ny)
+            return jnp.concatenate([keep[:, :, first : first + HALO], got[:, :, first : first + HALO]], axis=0)
 
         first, last = edge(0), edge(rows - HALO)
         m_low = lax.ppermute(last, "tile", up)
@@ -506,17 +512,19 @@
         pairs, ends = pl.pallas_call(
             functools.partial(pair_kernel, scale),
             in_specs=[VM, VM],
-            out_specs=[VM, VM],
+            out_specs=[HBM, VM],
             out_shape=[
                 struct((len(POINTS), BY, rows, 128), F32),
                 struct((2 * count, BY // 2, 16, 128), BF16),
             ],
             scratch_shapes=[
+                pltpu.VMEM((len(POINTS), BY, rows, 128), F32),
                 pltpu.VMEM((2 * count, BY, rows + 16, 128), F32),
                 pltpu.VMEM((2 * count, BY + 2 * HALO, rows, 128), F32),
                 pltpu.VMEM((2 * count * 2 * rows, ny), F32),
-            ],
-            compiler_params=vmem(10),
+                pltpu.SemaphoreType.DMA,
+            ],
+            compiler_params=pltpu.CompilerParams(vmem_limit_bytes=PAIRS_KIB << 10),
             cost_estimate=cost(8),
         )(keep, got)
 
@@ -535,7 +543,7 @@
                 pltpu.VMEM((256, 8 * 128), BF16),
             ],
             compiler_params=vmem(),
-        )(recv, pairs)
+        )(recv, ends)
     with jax.named_scope("spread_edges"):
         s_low = lax.ppermute(f_high, "tile", up)
         s_high = lax.ppermute(f_low, "tile", down)

time: 80.8 us -> 77.9 us (0.964)
  local copies, waits for them, and re-layouts: 6.33 us -> 3.9 us
  waiting for transfers between devices: 7.64 us -> 9.95 us
  starting transfers between devices: 23.5 us -> 21.6 us
    all_to_all x1, waiting for transfers between devices: 0.01 us -> 2.29 us  [on_device(): recv = lax.all_to_all(sent, 'tile', 0, 0, tiled=True)]
    ppermute x1, starting transfers between devices: 3.14 us -> 1.45 us  [on_device(): s_high = lax.ppermute(f_low, 'tile', down)]
    reshape x2 -> x0, local copies, waits for them, and re-layouts: 1.4 us -> none  [edge(): return both.transpose(1, 0, 2, 3).reshape(2, 2 * count * HALO, ny)]
    unnamed x14 -> x8, local copies, waits for them, and re-layouts: 2.67 us -> 1.77 us
    pallas_call x1, Pallas kernels: 3.47 us -> 2.63 us  [on_device(): pl.pallas_call(functools.partial(pair_edge_kernel, scale), in_specs=[VM,...]
  transfers between devices with their start and end apart: 9 -> 9, of which waited for: 3 -> 4; matrix products, arithmetic and copies ran while one was open for 4% -> 2% of each run, Pallas kernels for 22% -> 23%
where the time goes in v2:
time: 77.9 us; the launch traced here: 77.6 us
  Pallas kernels  22.6 us (29%)
  starting transfers between devices  21.6 us (28%)
  blocking collectives  18.5 us (24%)
  waiting for transfers between devices  9.95 us (13%)
  local copies, waits for them, and re-layouts  3.9 us (5%)
  between operations  0.82 us (1%)
    all_to_all x1, blocking collectives, on_device(): back = lax.all_to_all(back, 'tile', 0, 0, tiled=True)  18.5 us
    all_to_all x1, starting transfers between devices, on_device(): recv = lax.all_to_all(sent, 'tile', 0, 0, tiled=True)  8.17 us
    pallas_call x1, Pallas kernels, on_device(): pl.pallas_call(functools.partial(pair_kernel, scale), in_specs=[VM, VM],...  7.77 us
    ppermute x2, waiting for transfers between devices, on_device(): lax.ppermute(parts, 'mem', [(m, m ^ step) for m in range(n_groups)])  5.53 us
    pallas_call x1, Pallas kernels, on_device(): pl.pallas_call(pack_kernel, in_specs=[SM] + [HBM] * 5, out_specs=[VM] * 3...  5.43 us
    ppermute x1, starting transfers between devices, on_device(): lax.ppermute(parts, 'mem', [(m, n_groups - 1 - m) for m in range(n_groups)])  4.65 us
    pallas_call x1, Pallas kernels, on_device(): pl.pallas_call(image_kernel, in_specs=[VM] * 6, out_specs=VM, out_shape=s...  3.28 us
    ppermute x2, starting transfers between devices, on_device(): lax.ppermute(parts, 'mem', [(m, m ^ step) for m in range(n_groups)])  2.9 us
  transfers between devices with their start and end apart: 9, of which 4 were waited for; matrix products, arithmetic and copies ran while one was open for 2% of the time, Pallas kernels for 23%

profile of v2, /device:TPU:1, one launch (start us, length us, event | category | flops | bytes accessed | tf_op | source)
XLA Modules:
  0.0 77.6 jit_solution(3559678188362097745)
XLA Ops:
  0.6 1.0 %constant_dynamic-slice_fusion = bf16[10,2,16,512]{3,2,1,0:T(8,128)(2,1)S(1)} fusion(bf16[10,4,16,512]{3,2,1,0:T(8,128)(2,1)} %members_any.1, s32[]{:T(128)S(6)} %select_n.11), kind=kLoop, calls=%fused_computation.2 | loop fusion | bytes 655364 | tf_op jit(solution)/shard_map/swap/dynamic_slice | solution.py:473
  1.7 2.6 %collective-permute-start = (bf16[10,2,16,512]{3,2,1,0:T(8,128)(2,1)S(1)}, bf16[10,2,16,512]{3,2,1,0:T(8,128)(2,1)S(1)}, u32[]{:S(2)}, u32[]{:S(2)}) collective-permute-start(bf16[10,2,16,512]{3,2,1,0:T(8,128)(2,1)S(1)} %constant_dynamic-slice_fusion), channel_id=1, source_target_pairs={{0,1},{1,0},{2,3},{3,2},{4,5},{5,4},{6,7},{7,6},{8,9},{9,8},{10,11... | collective-permute-start | bytes 983048 | tf_op jit(solution)/shard_map/swap/ppermute | solution.py:474
  4.2 5.4 %pack.1 = (bf16[32,80,128]{2,1,0:T(8,128)(2,1)}, bf16[128,2048]{1,0:T(8,128)(2,1)}, bf16[10,2,16,512]{3,2,1,0:T(8,128)(2,1)}) custom-call(s32[1]{0:T(128)} %bitcast.half_ref, bf16[2048,128]{1,0:T(8,128)(2,1)} %w_any.1, f32[4,2048]{1,0:T(4,128)} %modes_any.1, s32[1,2048]{1,0:T(1,128)} %bitcast.3, s32[1,2048]{1,0:T(1,128)} %bitcast.5, ...), custom_call_target="tpu_custom_call" | custom-call | tf_op jit(solution)/shard_map/pack/pallas_call | solution.py:476
  9.6 0.0 copy-start.1
  9.7 8.2 %all-to-all-start = ((bf16[32,80,128]{2,1,0:T(8,128)(2,1)}), bf16[32,80,128]{2,1,0:T(8,128)(2,1)S(1)}, u32[]{:S(2)}, u32[]{:S(2)}) async-start(bf16[32,80,128]{2,1,0:T(8,128)(2,1)} %get-tuple-element.10), calls=%async_computation | async-start | bytes 1310720 | tf_op jit(solution)/shard_map/forward/all_to_all | solution.py:499
  17.8 1.1 %fusion = (bf16[10,2,4,512]{3,2,1,0:T(4,128)(2,1)S(1)}, bf16[10,2,4,512]{3,2,1,0:T(4,128)(2,1)S(1)}) fusion(bf16[10,2,16,512]{3,2,1,0:T(8,128)(2,1)} %get-tuple-element.11.keep_ref), kind=kLoop, calls=%fused_computation.3 | loop fusion | bytes 327680 | tf_op jit(solution)/shard_map/member_edges/slice | solution.py:505
  18.9 0.0 collective-permute-done.got_ref
  18.9 0.1 fusion.1
  19.0 0.1 pad_maximum_fusion
  19.1 1.7 %collective-permute-start.3 = (bf16[20,2,4,512]{3,2,1,0:T(4,128)(2,1)S(1)}, bf16[20,2,4,512]{3,2,1,0:T(4,128)(2,1)S(1)}, u32[]{:S(2)}, u32[]{:S(2)}) collective-permute-start(bf16[20,2,4,512]{3,2,1,0:T(4,128)(2,1)S(1)} %pad_maximum_fusion), channel_id=1, source_target_pairs={{0,8},{8,16},{16,24},{24,32},{32,40},{40,48},{48,56},{56,64},{64,7... | collective-permute-start | bytes 491528 | tf_op jit(solution)/shard_map/member_edges/ppermute | solution.py:508
  20.8 0.1 pad_maximum_fusion.1
  20.9 0.1 collective-permute-start.4
  21.0 0.0 copy-done.1
  21.0 7.8 %pairs.1 = (f32[41,8,16,128]{3,2,1,0:T(8,128)}, bf16[20,4,16,128]{3,2,1,0:T(8,128)(2,1)S(1)}) custom-call(bf16[10,2,16,512]{3,2,1,0:T(8,128)(2,1)S(1)} %copy-done.1, bf16[10,2,16,512]{3,2,1,0:T(8,128)(2,1)S(1)} %collective-permute-done.got_ref), custom_call_target="tpu_custom_call" | custom-call | bytes 29520000 | tf_op jit(solution)/shard_map/pairs/pallas_call | solution.py:512
  28.8 2.3 %all-to-all-done.recv_ref = bf16[32,80,128]{2,1,0:T(8,128)(2,1)S(1)} async-done(((bf16[32,80,128]{2,1,0:T(8,128)(2,1)}), bf16[32,80,128]{2,1,0:T(8,128)(2,1)S(1)}, u32[]{:S(2)}, u32[]{:S(2)}) %all-to-all-start) | async-done | bytes 655392 | tf_op jit(solution)/shard_map/forward/all_to_all | solution.py:499
  31.1 2.1 %spread.1 = (f32[32,16,128]{2,1,0:T(8,128)S(1)}, f32[128,128]{1,0:T(8,128)S(1)}, f32[128,128]{1,0:T(8,128)S(1)}) custom-call(bf16[32,80,128]{2,1,0:T(8,128)(2,1)S(1)} %all-to-all-done.recv_ref, bf16[20,4,16,128]{3,2,1,0:T(8,128)(2,1)S(1)} %get-tuple-element.12.after_ref.ends_ref), custom_call_target="tpu_custom_call" | custom-call | tf_op jit(solution)/shard_map/spread/pallas_call | solution.py:532
  33.2 0.1 collective-permute-start.1
  33.3 1.4 %collective-permute-start.2 = (f32[128,128]{1,0:T(8,128)S(1)}, f32[128,128]{1,0:T(8,128)S(1)}, u32[]{:S(2)}, u32[]{:S(2)}) collective-permute-start(f32[128,128]{1,0:T(8,128)S(1)} %get-tuple-element.15.after_ref), channel_id=1, source_target_pairs={{8,0},{16,8},{24,16},{32,24},{40,32},{48,40},{56,48},{64,56},{72,6... | collective-permute-start | bytes 196616 | tf_op jit(solution)/shard_map/spread_edges/ppermute | solution.py:549
  34.7 0.0 collective-permute-done.3.low_ref
  34.7 0.0 collective-permute-done.4.high_ref
  34.7 0.0 copy-start.2
  34.8 0.0 copy-start.3
  34.8 2.6 %pair_edges.1.ce_ref = f32[16,8,8,128]{3,2,1,0:T(8,128)S(1)} custom-call(bf16[20,4,16,128]{3,2,1,0:T(8,128)(2,1)S(1)} %get-tuple-element.12.after_ref.ends_ref, bf16[20,2,4,512]{3,2,1,0:T(4,128)(2,1)S(1)} %collective-permute-done.3.low_ref, bf16[20,2,4,512]{3,2,1,0:T(4,128)(2,1)S(1)} %collective-permute-done.4.high_ref, ...), custom_call_target="tpu_custom_call" | custom-call | bytes 11070000 | tf_op jit(solution)/shard_map/pair_edges/pallas_call | solution.py:551
  37.4 0.0 collective-permute-done.1.low_ref
  37.4 0.0 collective-permute-done.2.high_ref
  37.4 0.0 copy-start
  37.4 1.7 %copy-done = f32[41,8,16,128]{3,2,1,0:T(8,128)S(1)} copy-done((f32[41,8,16,128]{3,2,1,0:T(8,128)S(1)}, f32[41,8,16,128]{3,2,1,0:T(8,128)}, u32[]{:S(2)}) %copy-start) | copy-done | bytes 2687000
  39.2 3.3 %images.1 = f32[17,8,128]{2,1,0:T(8,128)S(1)} custom-call(bf16[32,80,128]{2,1,0:T(8,128)(2,1)S(1)} %all-to-all-done.recv_ref, f32[32,16,128]{2,1,0:T(8,128)S(1)} %get-tuple-element.13.f_ref, f32[128,128]{1,0:T(8,128)S(1)} %collective-permute-done.1.low_ref, f32[128,128]{1,0:T(8,128)S(1)} %collective-permute-done.2.high_ref, f32[41,8,16,128]{3,2,1,0:T(8,128)S(1)} %copy-done, ...), custom_call_target="tpu_custom_call" | custom-call | tf_op jit(solution)/shard_map/images/pallas_call | solution.py:565
  42.5 0.1 collective-permute-start.5
  42.6 3.1 %collective-permute-done.5 = f32[17,8,128]{2,1,0:T(8,128)S(1)} collective-permute-done((f32[17,8,128]{2,1,0:T(8,128)S(1)}, f32[17,8,128]{2,1,0:T(8,128)S(1)}, u32[]{:S(2)}, u32[]{:S(2)}) %collective-permute-start.5) | collective-permute-done | bytes 69664 | tf_op jit(solution)/shard_map/group_sum/ppermute | solution.py:580
  45.7 2.8 %collective-permute-start.6 = (f32[17,8,128]{2,1,0:T(8,128)S(1)}, f32[17,8,128]{2,1,0:T(8,128)S(1)}, u32[]{:S(2)}, u32[]{:S(2)}) collective-permute-start(f32[17,8,128]{2,1,0:T(8,128)S(1)} %add.16), channel_id=1, source_target_pairs={{0,3},{1,2},{2,1},{3,0},{4,7},{5,6},{6,5},{7,4},{8,11},{9,10},{10,... | collective-permute-start | bytes 208904 | tf_op jit(solution)/shard_map/group_sum/ppermute | solution.py:580
  48.5 2.4 %collective-permute-done.6 = f32[17,8,128]{2,1,0:T(8,128)S(1)} collective-permute-done((f32[17,8,128]{2,1,0:T(8,128)S(1)}, f32[17,8,128]{2,1,0:T(8,128)S(1)}, u32[]{:S(2)}, u32[]{:S(2)}) %collective-permute-start.6) | collective-permute-done | bytes 69664 | tf_op jit(solution)/shard_map/group_sum/ppermute | solution.py:580
  50.9 4.6 %collective-permute-start.7 = (f32[17,8,128]{2,1,0:T(8,128)S(1)}, f32[17,8,128]{2,1,0:T(8,128)S(1)}, u32[]{:S(2)}, u32[]{:S(2)}) collective-permute-start(f32[17,8,128]{2,1,0:T(8,128)S(1)} %add.17.parts_ref), channel_id=1, source_target_pairs={{0,7},{1,6},{2,5},{3,4},{4,3},{5,2},{6,1},{7,0},{8,15},{9,14},{10,... | collective-permute-start | bytes 208904 | tf_op jit(solution)/shard_map/group_sum/ppermute | solution.py:581
  55.6 2.1 %collective-permute-done.7.other_ref = f32[17,8,128]{2,1,0:T(8,128)S(1)} collective-permute-done((f32[17,8,128]{2,1,0:T(8,128)S(1)}, f32[17,8,128]{2,1,0:T(8,128)S(1)}, u32[]{:S(2)}, u32[]{:S(2)}) %collective-permute-start.7) | collective-permute-done | bytes 69664 | tf_op jit(solution)/shard_map/group_sum/ppermute | solution.py:581
  57.7 0.1 gram.1
  57.8 18.5 %all_to_all.10.back_ref = f32[32,8,128]{2,1,0:T(8,128)S(1)} all-to-all(f32[32,8,128]{2,1,0:T(8,128)S(1)} %gram.1), channel_id=1, replica_groups=mesh['tile'=32,'mem'=8] {'tile'}, dimensions={0} | all-to-all | bytes 262144 | tf_op jit(solution)/shard_map/return/all_to_all | solution.py:591
  76.3 0.0 copy-done.2
  76.3 0.0 copy-done.3
  76.3 1.3 %finish.1 = (f32[4,2048]{1,0:T(4,128)}, f32[4]{0:T(128)}) custom-call(f32[32,8,128]{2,1,0:T(8,128)S(1)} %all_to_all.10.back_ref, bf16[128,2048]{1,0:T(8,128)(2,1)S(1)} %copy-done.2, s32[1,2048]{1,0:T(1,128)S(1)} %bitcast.4), custom_call_target="tpu_custom_call" | custom-call | tf_op jit(solution)/shard_map/finish/pallas_call | solution.py:593
  (2 shorter events, 0.0 us)
Async XLA Ops:
  1.7 17.2 %collective-permute-start = (bf16[10,2,16,512]{3,2,1,0:T(8,128)(2,1)S(1)}, bf16[10,2,16,512]{3,2,1,0:T(8,128)(2,1)S(1)}, u32[]{:S(2)}, u32[]{:S(2)}) collective-permute-start(bf16[10,2,16,512]{3,2,1,0:T(8,128)(2,1)S(1)} %constant_dynamic-slice_fusion), channel_id=1, source_target_pairs={{0,1},{1,0},{2,3},{3,2},{4,5},{5,4},{6,7},{7,6},{8,9},{9,8},{10,11... | collective-permute-start | bytes 983048 | tf_op jit(solution)/shard_map/swap/ppermute | solution.py:474
  9.6 11.4 %copy-start.1 = (bf16[10,2,16,512]{3,2,1,0:T(8,128)(2,1)S(1)}, bf16[10,2,16,512]{3,2,1,0:T(8,128)(2,1)}, u32[]{:S(2)}) copy-start(bf16[10,2,16,512]{3,2,1,0:T(8,128)(2,1)} %get-tuple-element.11.keep_ref) | copy-start | bytes 983044
  9.7 21.4 %all-to-all-start = ((bf16[32,80,128]{2,1,0:T(8,128)(2,1)}), bf16[32,80,128]{2,1,0:T(8,128)(2,1)S(1)}, u32[]{:S(2)}, u32[]{:S(2)}) async-start(bf16[32,80,128]{2,1,0:T(8,128)(2,1)} %get-tuple-element.10), calls=%async_computation | async-start | bytes 1310720 | tf_op jit(solution)/shard_map/forward/all_to_all | solution.py:499
  19.1 15.6 %collective-permute-start.3 = (bf16[20,2,4,512]{3,2,1,0:T(4,128)(2,1)S(1)}, bf16[20,2,4,512]{3,2,1,0:T(4,128)(2,1)S(1)}, u32[]{:S(2)}, u32[]{:S(2)}) collective-permute-start(bf16[20,2,4,512]{3,2,1,0:T(4,128)(2,1)S(1)} %pad_maximum_fusion), channel_id=1, source_target_pairs={{0,8},{8,16},{16,24},{24,32},{32,40},{40,48},{48,56},{56,64},{64,7... | collective-permute-start | bytes 491528 | tf_op jit(solution)/shard_map/member_edges/ppermute | solution.py:508
  20.9 13.8 %collective-permute-start.4 = (bf16[20,2,4,512]{3,2,1,0:T(4,128)(2,1)S(1)}, bf16[20,2,4,512]{3,2,1,0:T(4,128)(2,1)S(1)}, u32[]{:S(2)}, u32[]{:S(2)}) collective-permute-start(bf16[20,2,4,512]{3,2,1,0:T(4,128)(2,1)S(1)} %pad_maximum_fusion.1), channel_id=1, source_target_pairs={{8,0},{16,8},{24,16},{32,24},{40,32},{48,40},{56,48},{64,56},{72,6... | collective-permute-start | bytes 491528 | tf_op jit(solution)/shard_map/member_edges/ppermute | solution.py:509
  33.2 4.2 %collective-permute-start.1 = (f32[128,128]{1,0:T(8,128)S(1)}, f32[128,128]{1,0:T(8,128)S(1)}, u32[]{:S(2)}, u32[]{:S(2)}) collective-permute-start(f32[128,128]{1,0:T(8,128)S(1)} %get-tuple-element.14), channel_id=1, source_target_pairs={{0,8},{8,16},{16,24},{24,32},{32,40},{40,48},{48,56},{56,64},{64,7... | collective-permute-start | bytes 196616 | tf_op jit(solution)/shard_map/spread_edges/ppermute | solution.py:548
  33.3 4.1 %collective-permute-start.2 = (f32[128,128]{1,0:T(8,128)S(1)}, f32[128,128]{1,0:T(8,128)S(1)}, u32[]{:S(2)}, u32[]{:S(2)}) collective-permute-start(f32[128,128]{1,0:T(8,128)S(1)} %get-tuple-element.15.after_ref), channel_id=1, source_target_pairs={{8,0},{16,8},{24,16},{32,24},{40,32},{48,40},{56,48},{64,56},{72,6... | collective-permute-start | bytes 196616 | tf_op jit(solution)/shard_map/spread_edges/ppermute | solution.py:549
  34.7 41.6 %copy-start.2 = (bf16[128,2048]{1,0:T(8,128)(2,1)S(1)}, bf16[128,2048]{1,0:T(8,128)(2,1)}, u32[]{:S(2)}) copy-start(bf16[128,2048]{1,0:T(8,128)(2,1)} %get-tuple-element.17.hot_ref) | copy-start | bytes 1572868
  34.8 41.6 %copy-start.3 = (s32[2048,1]{0,1:T(1,128)S(1)}, s32[2048,1]{0,1:T(1,128)}, u32[]{:S(2)}) copy-start(s32[2048,1]{0,1:T(1,128)} %param.8) | copy-start | bytes 24580
  37.4 1.8 %copy-start = (f32[41,8,16,128]{3,2,1,0:T(8,128)S(1)}, f32[41,8,16,128]{3,2,1,0:T(8,128)}, u32[]{:S(2)}) copy-start(f32[41,8,16,128]{3,2,1,0:T(8,128)} %get-tuple-element.16.c_ref) | copy-start | bytes 8060932
  42.5 3.2 %collective-permute-start.5 = (f32[17,8,128]{2,1,0:T(8,128)S(1)}, f32[17,8,128]{2,1,0:T(8,128)S(1)}, u32[]{:S(2)}, u32[]{:S(2)}) collective-permute-start(f32[17,8,128]{2,1,0:T(8,128)S(1)} %images.1), channel_id=1, source_target_pairs={{0,1},{1,0},{2,3},{3,2},{4,5},{5,4},{6,7},{7,6},{8,9},{9,8},{10,11... | collective-permute-start | bytes 208904 | tf_op jit(solution)/shard_map/group_sum/ppermute | solution.py:580
  45.7 5.2 %collective-permute-start.6 = (f32[17,8,128]{2,1,0:T(8,128)S(1)}, f32[17,8,128]{2,1,0:T(8,128)S(1)}, u32[]{:S(2)}, u32[]{:S(2)}) collective-permute-start(f32[17,8,128]{2,1,0:T(8,128)S(1)} %add.16), channel_id=1, source_target_pairs={{0,3},{1,2},{2,1},{3,0},{4,7},{5,6},{6,5},{7,4},{8,11},{9,10},{10,... | collective-permute-start | bytes 208904 | tf_op jit(solution)/shard_map/group_sum/ppermute | solution.py:580
  50.9 6.8 %collective-permute-start.7 = (f32[17,8,128]{2,1,0:T(8,128)S(1)}, f32[17,8,128]{2,1,0:T(8,128)S(1)}, u32[]{:S(2)}, u32[]{:S(2)}) collective-permute-start(f32[17,8,128]{2,1,0:T(8,128)S(1)} %add.17.parts_ref), channel_id=1, source_target_pairs={{0,7},{1,6},{2,5},{3,4},{4,3},{5,2},{6,1},{7,0},{8,15},{9,14},{10,... | collective-permute-start | bytes 208904 | tf_op jit(solution)/shard_map/group_sum/ppermute | solution.py:581

commit v3 on v2

--- a/solution.py
+++ b/solution.py
@@ -34,6 +34,7 @@
 EDGE_POINTS = [p for p in POINTS if p[0] > 0]
 EDGE_POINTS = [(dx, dy, n, i) for i, (dx, dy, n, _) in enumerate(EDGE_POINTS)]
 TOTAL = float(5**STEPS)
+CUT = len([p for p in POINTS if p[0] <= 0])
 
 PAIRS_KIB = 65536 - 12000
 
@@ -117,7 +118,7 @@
             out_ref[pl.ds(first, group)] = sent.astype(BF16).reshape(group, ROWS, 128)
         return carry
 
-    lax.fori_loop(0, n_tiles // (2 * group), send, 0)
+    lax.fori_loop(0, n_tiles // (2 * group), send, 0, unroll=True)
 
 
 def extend(ext_ref, lead):
@@ -161,7 +162,7 @@
 
 
 def pair_kernel(
-    scale, keep_ref, got_ref, out_any, ends_ref, out_ref, center_ref, ext_ref, y_ref, sem
+    scale, keep_ref, got_ref, behind_any, ahead_any, ends_ref, out_ref, center_ref, ext_ref, y_ref, sems
 ):
     count = got_ref.shape[0]
     total = 2 * count
@@ -199,11 +200,13 @@
                 return center_ref[m, c, 8 + v * 8 - dx : 16 + v * 8 - dx, :]
 
             pair_sums(center_of, ext_ref, out_ref, scale, c, v * 8, POINTS)
-        pltpu.make_async_copy(out_ref.at[:, c], out_any.at[:, c], sem).start()
+        pltpu.make_async_copy(out_ref.at[0:CUT, c], behind_any.at[:, c], sems.at[0]).start()
+        pltpu.make_async_copy(out_ref.at[CUT:, c], ahead_any.at[:, c], sems.at[1]).start()
         return carry
 
     lax.fori_loop(0, BY, plane, 0)
-    pltpu.make_async_copy(out_ref, out_any, sem).wait()
+    pltpu.make_async_copy(out_ref.at[0:CUT], behind_any, sems.at[0]).wait()
+    pltpu.make_async_copy(out_ref.at[CUT:], ahead_any, sems.at[1]).wait()
 
 
 def pair_edge_kernel(scale, ends_ref, low_ref, high_ref, after_ref, out_ref, center_ref, ext_ref, y_ref):
@@ -269,7 +272,7 @@
                     g_ref[row : row + 32, at] = (w[l * 32 : l * 32 + 32, :] * tail[k : k + 1, :]).astype(BF16)
         return total + matmul(g_ref[...], h_ref[...], NT)
 
-    r = lax.fori_loop(0, n_tiles // group, sources, jnp.zeros((256, 256), F32))
+    r = lax.fori_loop(0, n_tiles // group, sources, jnp.zeros((256, 256), F32), unroll=2)
     for i in range(4):
         t = jnp.concatenate([r[0:128, i * 64 : i * 64 + 64], r[128:256, i * 64 : i * 64 + 64]], axis=1)
         if i == 0:
@@ -280,7 +283,7 @@
             out_ref[n, i * 4 : i * 4 + 4, :] = t[n * 4 : n * 4 + 4, :]
 
 
-def image_kernel(recv_ref, f_ref, low_ref, high_ref, c_ref, ce_ref, out_ref, ext_ref, side_ref, q_ref, t_ref):
+def image_kernel(recv_ref, f_ref, low_ref, high_ref, behind_ref, ahead_ref, ce_ref, out_ref, ext_ref, side_ref, q_ref, t_ref):
     n_tiles = recv_ref.shape[0]
     rows = f_ref.shape[1]
     for k in range(MODES):
@@ -295,7 +298,7 @@
     def weigh(ref, v, c, points, weights):
         sums = [{} for _ in range(MODES)]
         for dx, dy, n, i in points:
-            weight = weights[i, c, v * 8 : v * 8 + 8, :]
+            weight = weights(i)[c, v * 8 : v * 8 + 8, :]
             for k in range(MODES):
                 term = weight * ref[k, HALO + c + dy, v * 8 : v * 8 + 8, :]
                 sums[k][dx] = sums[k][dx] + term if dx in sums[k] else term
@@ -305,10 +308,10 @@
         for j in range(2):
             c = 2 * cp + j
             for v in range(rows // 8):
-                for k, sums in enumerate(weigh(ext_ref, v, c, POINTS, c_ref)):
+                for k, sums in enumerate(weigh(ext_ref, v, c, POINTS, lambda i: behind_ref.at[i] if i < CUT else ahead_ref.at[i - CUT])):
                     for dx, q in sums.items():
                         q_ref[k, j, dx + HALO, 8 + v * 8 : 16 + v * 8, :] = q
-            for k, sums in enumerate(weigh(side_ref, 0, c, EDGE_POINTS, ce_ref)):
+            for k, sums in enumerate(weigh(side_ref, 0, c, EDGE_POINTS, lambda i: ce_ref.at[i])):
                 for dx, q in sums.items():
                     q_ref[k, j, HALO - dx, 0:8, :] = q
                     q_ref[k, j, HALO + dx, rows + 8 : rows + 16, :] = q
@@ -360,7 +363,7 @@
         return cross, square
 
     zero = jnp.zeros((MODES, 128), F32)
-    cross, square = lax.fori_loop(0, n_tiles // group, image, (zero, zero))
+    cross, square = lax.fori_loop(0, n_tiles // group, image, (zero, zero), unroll=2)
     out_ref[n_tiles // 2, 0:4, :] = cross
     out_ref[n_tiles // 2, 4:8, :] = square
 
@@ -509,12 +512,13 @@
         m_high = lax.ppermute(first, "tile", down)
     scale = 1.0 / (TOTAL * (count * n_groups - 1))
     with jax.named_scope("pairs"):
-        pairs, ends = pl.pallas_call(
+        behind, ahead, ends = pl.pallas_call(
             functools.partial(pair_kernel, scale),
             in_specs=[VM, VM],
-            out_specs=[HBM, VM],
+            out_specs=[HBM, HBM, VM],
             out_shape=[
-                struct((len(POINTS), BY, rows, 128), F32),
+                struct((CUT, BY, rows, 128), F32),
+                struct((len(POINTS) - CUT, BY, rows, 128), F32),
                 struct((2 * count, BY // 2, 16, 128), BF16),
             ],
             scratch_shapes=[
@@ -522,7 +526,7 @@
                 pltpu.VMEM((2 * count, BY, rows + 16, 128), F32),
                 pltpu.VMEM((2 * count, BY + 2 * HALO, rows, 128), F32),
                 pltpu.VMEM((2 * count * 2 * rows, ny), F32),
-                pltpu.SemaphoreType.DMA,
+                pltpu.SemaphoreType.DMA((2,)),
             ],
             compiler_params=pltpu.CompilerParams(vmem_limit_bytes=PAIRS_KIB << 10),
             cost_estimate=cost(8),
@@ -564,7 +568,7 @@
     with jax.named_scope("images"):
         parts = pl.pallas_call(
             image_kernel,
-            in_specs=[VM] * 6,
+            in_specs=[VM] * 7,
             out_specs=VM,
             out_shape=struct((n_tiles // 2 + 1, 8, 128), F32),
             scratch_shapes=[
@@ -574,7 +578,7 @@
                 pltpu.VMEM((4, 128, 128), F32),
             ],
             compiler_params=vmem(),
-        )(recv, field, s_low, s_high, pairs, pairs_edge)
+        )(recv, field, s_low, s_high, behind, ahead, pairs_edge)
     with jax.named_scope("group_sum"):
         for step in (1, 3):
             parts = parts + lax.ppermute(parts, "mem", [(m, m ^ step) for m in range(n_groups)])

time: 77.9 us -> 76.4 us (0.981)
  Pallas kernels: 22.6 us -> 21.6 us
    unnamed x8 -> x10, local copies, waits for them, and re-layouts: 1.77 us -> 1.23 us
where the time goes in v3:
time: 76.4 us; the launch traced here: 76.1 us
  starting transfers between devices  21.6 us (28%)
  Pallas kernels  21.6 us (28%)
  blocking collectives  18.5 us (24%)
  waiting for transfers between devices  9.97 us (13%)
  local copies, waits for them, and re-layouts  3.37 us (4%)
  between operations  0.82 us (1%)
    all_to_all x1, blocking collectives, on_device(): back = lax.all_to_all(back, 'tile', 0, 0, tiled=True)  18.5 us
    all_to_all x1, starting transfers between devices, on_device(): recv = lax.all_to_all(sent, 'tile', 0, 0, tiled=True)  8.17 us
    pallas_call x1, Pallas kernels, on_device(): pl.pallas_call(functools.partial(pair_kernel, scale), in_specs=[VM, VM],...  7.76 us
    ppermute x2, waiting for transfers between devices, on_device(): lax.ppermute(parts, 'mem', [(m, m ^ step) for m in range(n_groups)])  5.55 us
    pallas_call x1, Pallas kernels, on_device(): pl.pallas_call(pack_kernel, in_specs=[SM] + [HBM] * 5, out_specs=[VM] * 3...  5.11 us
    ppermute x1, starting transfers between devices, on_device(): lax.ppermute(parts, 'mem', [(m, n_groups - 1 - m) for m in range(n_groups)])  4.64 us
    pallas_call x1, Pallas kernels, on_device(): pl.pallas_call(image_kernel, in_specs=[VM] * 7, out_specs=VM, out_shape=s...  2.89 us
    ppermute x2, starting transfers between devices, on_device(): lax.ppermute(parts, 'mem', [(m, m ^ step) for m in range(n_groups)])  2.89 us
  transfers between devices with their start and end apart: 9, of which 4 were waited for; matrix products, arithmetic and copies ran while one was open for 2% of the time, Pallas kernels for 23%

profile of v3, /device:TPU:1, one launch (start us, length us, event | category | flops | bytes accessed | tf_op | source)
XLA Modules:
  0.0 76.1 jit_solution(16909942454905865831)
XLA Ops:
  0.6 1.0 %constant_dynamic-slice_fusion = bf16[10,2,16,512]{3,2,1,0:T(8,128)(2,1)S(1)} fusion(bf16[10,4,16,512]{3,2,1,0:T(8,128)(2,1)} %members_any.1, s32[]{:T(128)S(6)} %select_n.11), kind=kLoop, calls=%fused_computation.2 | loop fusion | bytes 655364 | tf_op jit(solution)/shard_map/swap/dynamic_slice | solution.py:476
  1.7 2.6 %collective-permute-start = (bf16[10,2,16,512]{3,2,1,0:T(8,128)(2,1)S(1)}, bf16[10,2,16,512]{3,2,1,0:T(8,128)(2,1)S(1)}, u32[]{:S(2)}, u32[]{:S(2)}) collective-permute-start(bf16[10,2,16,512]{3,2,1,0:T(8,128)(2,1)S(1)} %constant_dynamic-slice_fusion), channel_id=1, source_target_pairs={{0,1},{1,0},{2,3},{3,2},{4,5},{5,4},{6,7},{7,6},{8,9},{9,8},{10,11... | collective-permute-start | bytes 983048 | tf_op jit(solution)/shard_map/swap/ppermute | solution.py:477
  4.2 5.1 %pack.1 = (bf16[32,80,128]{2,1,0:T(8,128)(2,1)}, bf16[128,2048]{1,0:T(8,128)(2,1)}, bf16[10,2,16,512]{3,2,1,0:T(8,128)(2,1)}) custom-call(s32[1]{0:T(128)} %bitcast.half_ref, bf16[2048,128]{1,0:T(8,128)(2,1)} %w_any.1, f32[4,2048]{1,0:T(4,128)} %modes_any.1, s32[1,2048]{1,0:T(1,128)} %bitcast.3, s32[1,2048]{1,0:T(1,128)} %bitcast.5, ...), custom_call_target="tpu_custom_call" | custom-call | tf_op jit(solution)/shard_map/pack/pallas_call | solution.py:479
  9.3 0.0 copy-start.2
  9.3 8.2 %all-to-all-start = ((bf16[32,80,128]{2,1,0:T(8,128)(2,1)}), bf16[32,80,128]{2,1,0:T(8,128)(2,1)S(1)}, u32[]{:S(2)}, u32[]{:S(2)}) async-start(bf16[32,80,128]{2,1,0:T(8,128)(2,1)} %get-tuple-element.11), calls=%async_computation | async-start | bytes 1310720 | tf_op jit(solution)/shard_map/forward/all_to_all | solution.py:502
  17.5 1.1 %fusion = (bf16[10,2,4,512]{3,2,1,0:T(4,128)(2,1)S(1)}, bf16[10,2,4,512]{3,2,1,0:T(4,128)(2,1)S(1)}) fusion(bf16[10,2,16,512]{3,2,1,0:T(8,128)(2,1)} %get-tuple-element.12.keep_ref), kind=kLoop, calls=%fused_computation.3 | loop fusion | bytes 327680 | tf_op jit(solution)/shard_map/member_edges/slice | solution.py:508
  18.6 0.0 collective-permute-done.got_ref
  18.6 0.1 fusion.1
  18.7 0.1 pad_maximum_fusion
  18.8 1.7 %collective-permute-start.3 = (bf16[20,2,4,512]{3,2,1,0:T(4,128)(2,1)S(1)}, bf16[20,2,4,512]{3,2,1,0:T(4,128)(2,1)S(1)}, u32[]{:S(2)}, u32[]{:S(2)}) collective-permute-start(bf16[20,2,4,512]{3,2,1,0:T(4,128)(2,1)S(1)} %pad_maximum_fusion), channel_id=1, source_target_pairs={{0,8},{8,16},{16,24},{24,32},{32,40},{40,48},{48,56},{56,64},{64,7... | collective-permute-start | bytes 491528 | tf_op jit(solution)/shard_map/member_edges/ppermute | solution.py:511
  20.5 0.1 pad_maximum_fusion.1
  20.6 0.1 collective-permute-start.4
  20.7 0.0 copy-done.2
  20.7 7.8 %pairs.1 = (f32[25,8,16,128]{3,2,1,0:T(8,128)}, f32[16,8,16,128]{3,2,1,0:T(8,128)}, bf16[20,4,16,128]{3,2,1,0:T(8,128)(2,1)S(1)}) custom-call(bf16[10,2,16,512]{3,2,1,0:T(8,128)(2,1)S(1)} %copy-done.2, bf16[10,2,16,512]{3,2,1,0:T(8,128)(2,1)S(1)} %collective-permute-done.got_ref), custom_call_target="tpu_custom_call" | custom-call | bytes 29520000 | tf_op jit(solution)/shard_map/pairs/pallas_call | solution.py:515
  28.5 0.0 copy-start
  28.5 2.3 %all-to-all-done.recv_ref = bf16[32,80,128]{2,1,0:T(8,128)(2,1)S(1)} async-done(((bf16[32,80,128]{2,1,0:T(8,128)(2,1)}), bf16[32,80,128]{2,1,0:T(8,128)(2,1)S(1)}, u32[]{:S(2)}, u32[]{:S(2)}) %all-to-all-start) | async-done | bytes 655392 | tf_op jit(solution)/shard_map/forward/all_to_all | solution.py:502
  30.8 1.8 %spread.1 = (f32[32,16,128]{2,1,0:T(8,128)S(1)}, f32[128,128]{1,0:T(8,128)S(1)}, f32[128,128]{1,0:T(8,128)S(1)}) custom-call(bf16[32,80,128]{2,1,0:T(8,128)(2,1)S(1)} %all-to-all-done.recv_ref, bf16[20,4,16,128]{3,2,1,0:T(8,128)(2,1)S(1)} %get-tuple-element.13.after_ref.ends_ref), custom_call_target="tpu_custom_call" | custom-call | tf_op jit(solution)/shard_map/spread/pallas_call | solution.py:536
  32.6 0.1 collective-permute-start.1
  32.7 1.4 %collective-permute-start.2 = (f32[128,128]{1,0:T(8,128)S(1)}, f32[128,128]{1,0:T(8,128)S(1)}, u32[]{:S(2)}, u32[]{:S(2)}) collective-permute-start(f32[128,128]{1,0:T(8,128)S(1)} %get-tuple-element.16.after_ref), channel_id=1, source_target_pairs={{8,0},{16,8},{24,16},{32,24},{40,32},{48,40},{56,48},{64,56},{72,6... | collective-permute-start | bytes 196616 | tf_op jit(solution)/shard_map/spread_edges/ppermute | solution.py:553
  34.1 0.0 collective-permute-done.3.low_ref
  34.1 0.0 collective-permute-done.4.high_ref
  34.1 2.6 %pair_edges.1.ce_ref = f32[16,8,8,128]{3,2,1,0:T(8,128)S(1)} custom-call(bf16[20,4,16,128]{3,2,1,0:T(8,128)(2,1)S(1)} %get-tuple-element.13.after_ref.ends_ref, bf16[20,2,4,512]{3,2,1,0:T(4,128)(2,1)S(1)} %collective-permute-done.3.low_ref, bf16[20,2,4,512]{3,2,1,0:T(4,128)(2,1)S(1)} %collective-permute-done.4.high_ref, ...), custom_call_target="tpu_custom_call" | custom-call | bytes 11070000 | tf_op jit(solution)/shard_map/pair_edges/pallas_call | solution.py:555
  36.8 0.0 collective-permute-done.1.low_ref
  36.8 0.0 collective-permute-done.2.high_ref
  36.8 0.0 copy-done
  36.8 0.0 copy-start.1
  36.8 1.2 %copy-done.1 = f32[16,8,16,128]{3,2,1,0:T(8,128)S(1)} copy-done((f32[16,8,16,128]{3,2,1,0:T(8,128)S(1)}, f32[16,8,16,128]{3,2,1,0:T(8,128)}, u32[]{:S(2)}) %copy-start.1) | copy-done | bytes 1048600
  38.0 0.0 copy-start.3
  38.0 0.0 copy-start.4
  38.0 2.9 %images.1 = f32[17,8,128]{2,1,0:T(8,128)S(1)} custom-call(bf16[32,80,128]{2,1,0:T(8,128)(2,1)S(1)} %all-to-all-done.recv_ref, f32[32,16,128]{2,1,0:T(8,128)S(1)} %get-tuple-element.14.f_ref, f32[128,128]{1,0:T(8,128)S(1)} %collective-permute-done.1.low_ref, f32[128,128]{1,0:T(8,128)S(1)} %collective-permute-done.2.high_ref, f32[25,8,16,128]{3,2,1,0:T(8,128)S(1)} %copy-done, ...), custom_call_target="tpu_custom_call" | custom-call | tf_op jit(solution)/shard_map/images/pallas_call | solution.py:569
  40.9 0.1 collective-permute-start.5
  41.0 3.1 %collective-permute-done.5 = f32[17,8,128]{2,1,0:T(8,128)S(1)} collective-permute-done((f32[17,8,128]{2,1,0:T(8,128)S(1)}, f32[17,8,128]{2,1,0:T(8,128)S(1)}, u32[]{:S(2)}, u32[]{:S(2)}) %collective-permute-start.5) | collective-permute-done | bytes 69664 | tf_op jit(solution)/shard_map/group_sum/ppermute | solution.py:584
  44.2 2.8 %collective-permute-start.6 = (f32[17,8,128]{2,1,0:T(8,128)S(1)}, f32[17,8,128]{2,1,0:T(8,128)S(1)}, u32[]{:S(2)}, u32[]{:S(2)}) collective-permute-start(f32[17,8,128]{2,1,0:T(8,128)S(1)} %add.16), channel_id=1, source_target_pairs={{0,3},{1,2},{2,1},{3,0},{4,7},{5,6},{6,5},{7,4},{8,11},{9,10},{10,... | collective-permute-start | bytes 208904 | tf_op jit(solution)/shard_map/group_sum/ppermute | solution.py:584
  47.0 2.4 %collective-permute-done.6 = f32[17,8,128]{2,1,0:T(8,128)S(1)} collective-permute-done((f32[17,8,128]{2,1,0:T(8,128)S(1)}, f32[17,8,128]{2,1,0:T(8,128)S(1)}, u32[]{:S(2)}, u32[]{:S(2)}) %collective-permute-start.6) | collective-permute-done | bytes 69664 | tf_op jit(solution)/shard_map/group_sum/ppermute | solution.py:584
  49.4 4.6 %collective-permute-start.7 = (f32[17,8,128]{2,1,0:T(8,128)S(1)}, f32[17,8,128]{2,1,0:T(8,128)S(1)}, u32[]{:S(2)}, u32[]{:S(2)}) collective-permute-start(f32[17,8,128]{2,1,0:T(8,128)S(1)} %add.17.parts_ref), channel_id=1, source_target_pairs={{0,7},{1,6},{2,5},{3,4},{4,3},{5,2},{6,1},{7,0},{8,15},{9,14},{10,... | collective-permute-start | bytes 208904 | tf_op jit(solution)/shard_map/group_sum/ppermute | solution.py:585
  54.0 2.1 %collective-permute-done.7.other_ref = f32[17,8,128]{2,1,0:T(8,128)S(1)} collective-permute-done((f32[17,8,128]{2,1,0:T(8,128)S(1)}, f32[17,8,128]{2,1,0:T(8,128)S(1)}, u32[]{:S(2)}, u32[]{:S(2)}) %collective-permute-start.7) | collective-permute-done | bytes 69664 | tf_op jit(solution)/shard_map/group_sum/ppermute | solution.py:585
  56.2 0.1 gram.1
  56.3 18.5 %all_to_all.10.back_ref = f32[32,8,128]{2,1,0:T(8,128)S(1)} all-to-all(f32[32,8,128]{2,1,0:T(8,128)S(1)} %gram.1), channel_id=1, replica_groups=mesh['tile'=32,'mem'=8] {'tile'}, dimensions={0} | all-to-all | bytes 262144 | tf_op jit(solution)/shard_map/return/all_to_all | solution.py:595
  74.8 0.0 copy-done.3
  74.8 0.0 copy-done.4
  74.8 1.3 %finish.1 = (f32[4,2048]{1,0:T(4,128)}, f32[4]{0:T(128)}) custom-call(f32[32,8,128]{2,1,0:T(8,128)S(1)} %all_to_all.10.back_ref, bf16[128,2048]{1,0:T(8,128)(2,1)S(1)} %copy-done.3, s32[1,2048]{1,0:T(1,128)S(1)} %bitcast.4), custom_call_target="tpu_custom_call" | custom-call | tf_op jit(solution)/shard_map/finish/pallas_call | solution.py:597
  (2 shorter events, 0.0 us)
Async XLA Ops:
  1.7 16.9 %collective-permute-start = (bf16[10,2,16,512]{3,2,1,0:T(8,128)(2,1)S(1)}, bf16[10,2,16,512]{3,2,1,0:T(8,128)(2,1)S(1)}, u32[]{:S(2)}, u32[]{:S(2)}) collective-permute-start(bf16[10,2,16,512]{3,2,1,0:T(8,128)(2,1)S(1)} %constant_dynamic-slice_fusion), channel_id=1, source_target_pairs={{0,1},{1,0},{2,3},{3,2},{4,5},{5,4},{6,7},{7,6},{8,9},{9,8},{10,11... | collective-permute-start | bytes 983048 | tf_op jit(solution)/shard_map/swap/ppermute | solution.py:477
  9.3 11.4 %copy-start.2 = (bf16[10,2,16,512]{3,2,1,0:T(8,128)(2,1)S(1)}, bf16[10,2,16,512]{3,2,1,0:T(8,128)(2,1)}, u32[]{:S(2)}) copy-start(bf16[10,2,16,512]{3,2,1,0:T(8,128)(2,1)} %get-tuple-element.12.keep_ref) | copy-start | bytes 983044
  9.3 21.5 %all-to-all-start = ((bf16[32,80,128]{2,1,0:T(8,128)(2,1)}), bf16[32,80,128]{2,1,0:T(8,128)(2,1)S(1)}, u32[]{:S(2)}, u32[]{:S(2)}) async-start(bf16[32,80,128]{2,1,0:T(8,128)(2,1)} %get-tuple-element.11), calls=%async_computation | async-start | bytes 1310720 | tf_op jit(solution)/shard_map/forward/all_to_all | solution.py:502
  18.8 15.4 %collective-permute-start.3 = (bf16[20,2,4,512]{3,2,1,0:T(4,128)(2,1)S(1)}, bf16[20,2,4,512]{3,2,1,0:T(4,128)(2,1)S(1)}, u32[]{:S(2)}, u32[]{:S(2)}) collective-permute-start(bf16[20,2,4,512]{3,2,1,0:T(4,128)(2,1)S(1)} %pad_maximum_fusion), channel_id=1, source_target_pairs={{0,8},{8,16},{16,24},{24,32},{32,40},{40,48},{48,56},{56,64},{64,7... | collective-permute-start | bytes 491528 | tf_op jit(solution)/shard_map/member_edges/ppermute | solution.py:511
  20.6 13.5 %collective-permute-start.4 = (bf16[20,2,4,512]{3,2,1,0:T(4,128)(2,1)S(1)}, bf16[20,2,4,512]{3,2,1,0:T(4,128)(2,1)S(1)}, u32[]{:S(2)}, u32[]{:S(2)}) collective-permute-start(bf16[20,2,4,512]{3,2,1,0:T(4,128)(2,1)S(1)} %pad_maximum_fusion.1), channel_id=1, source_target_pairs={{8,0},{16,8},{24,16},{32,24},{40,32},{48,40},{56,48},{64,56},{72,6... | collective-permute-start | bytes 491528 | tf_op jit(solution)/shard_map/member_edges/ppermute | solution.py:512
  28.5 8.3 %copy-start = (f32[25,8,16,128]{3,2,1,0:T(8,128)S(1)}, f32[25,8,16,128]{3,2,1,0:T(8,128)}, u32[]{:S(2)}) copy-start(f32[25,8,16,128]{3,2,1,0:T(8,128)} %get-tuple-element.17.behind_ref) | copy-start | bytes 4915204
  32.6 4.2 %collective-permute-start.1 = (f32[128,128]{1,0:T(8,128)S(1)}, f32[128,128]{1,0:T(8,128)S(1)}, u32[]{:S(2)}, u32[]{:S(2)}) collective-permute-start(f32[128,128]{1,0:T(8,128)S(1)} %get-tuple-element.15), channel_id=1, source_target_pairs={{0,8},{8,16},{16,24},{24,32},{32,40},{40,48},{48,56},{56,64},{64,7... | collective-permute-start | bytes 196616 | tf_op jit(solution)/shard_map/spread_edges/ppermute | solution.py:552
  32.7 4.1 %collective-permute-start.2 = (f32[128,128]{1,0:T(8,128)S(1)}, f32[128,128]{1,0:T(8,128)S(1)}, u32[]{:S(2)}, u32[]{:S(2)}) collective-permute-start(f32[128,128]{1,0:T(8,128)S(1)} %get-tuple-element.16.after_ref), channel_id=1, source_target_pairs={{8,0},{16,8},{24,16},{32,24},{40,32},{48,40},{56,48},{64,56},{72,6... | collective-permute-start | bytes 196616 | tf_op jit(solution)/shard_map/spread_edges/ppermute | solution.py:553
  36.8 1.2 %copy-start.1 = (f32[16,8,16,128]{3,2,1,0:T(8,128)S(1)}, f32[16,8,16,128]{3,2,1,0:T(8,128)}, u32[]{:S(2)}) copy-start(f32[16,8,16,128]{3,2,1,0:T(8,128)} %get-tuple-element.18.ahead_ref) | copy-start | bytes 3145732
  38.0 36.8 %copy-start.3 = (bf16[128,2048]{1,0:T(8,128)(2,1)S(1)}, bf16[128,2048]{1,0:T(8,128)(2,1)}, u32[]{:S(2)}) copy-start(bf16[128,2048]{1,0:T(8,128)(2,1)} %get-tuple-element.19.hot_ref) | copy-start | bytes 1572868
  38.0 36.8 %copy-start.4 = (s32[2048,1]{0,1:T(1,128)S(1)}, s32[2048,1]{0,1:T(1,128)}, u32[]{:S(2)}) copy-start(s32[2048,1]{0,1:T(1,128)} %param.8) | copy-start | bytes 24580
  40.9 3.2 %collective-permute-start.5 = (f32[17,8,128]{2,1,0:T(8,128)S(1)}, f32[17,8,128]{2,1,0:T(8,128)S(1)}, u32[]{:S(2)}, u32[]{:S(2)}) collective-permute-start(f32[17,8,128]{2,1,0:T(8,128)S(1)} %images.1), channel_id=1, source_target_pairs={{0,1},{1,0},{2,3},{3,2},{4,5},{5,4},{6,7},{7,6},{8,9},{9,8},{10,11... | collective-permute-start | bytes 208904 | tf_op jit(solution)/shard_map/group_sum/ppermute | solution.py:584
  44.2 5.2 %collective-permute-start.6 = (f32[17,8,128]{2,1,0:T(8,128)S(1)}, f32[17,8,128]{2,1,0:T(8,128)S(1)}, u32[]{:S(2)}, u32[]{:S(2)}) collective-permute-start(f32[17,8,128]{2,1,0:T(8,128)S(1)} %add.16), channel_id=1, source_target_pairs={{0,3},{1,2},{2,1},{3,0},{4,7},{5,6},{6,5},{7,4},{8,11},{9,10},{10,... | collective-permute-start | bytes 208904 | tf_op jit(solution)/shard_map/group_sum/ppermute | solution.py:584
  49.4 6.7 %collective-permute-start.7 = (f32[17,8,128]{2,1,0:T(8,128)S(1)}, f32[17,8,128]{2,1,0:T(8,128)S(1)}, u32[]{:S(2)}, u32[]{:S(2)}) collective-permute-start(f32[17,8,128]{2,1,0:T(8,128)S(1)} %add.17.parts_ref), channel_id=1, source_target_pairs={{0,7},{1,6},{2,5},{3,4},{4,3},{5,2},{6,1},{7,0},{8,15},{9,14},{10,... | collective-permute-start | bytes 208904 | tf_op jit(solution)/shard_map/group_sum/ppermute | solution.py:585

commit v4 on v3

--- a/solution.py
+++ b/solution.py
@@ -155,7 +155,7 @@
         return tuple(s + center[dx] * ext[dy] for s, (dx, dy, _, _) in zip(sums, points))
 
     sums = lax.fori_loop(
-        0, total, member, tuple(jnp.zeros((8, 128), F32) for _ in points), unroll=4
+        0, total, member, tuple(jnp.zeros((8, 128), F32) for _ in points), unroll=10
     )
     for s, (dx, dy, n, i) in zip(sums, points):
         out_ref[i, c, at : at + 8, :] = s * (n * scale)
@@ -272,7 +272,7 @@
                     g_ref[row : row + 32, at] = (w[l * 32 : l * 32 + 32, :] * tail[k : k + 1, :]).astype(BF16)
         return total + matmul(g_ref[...], h_ref[...], NT)
 
-    r = lax.fori_loop(0, n_tiles // group, sources, jnp.zeros((256, 256), F32), unroll=2)
+    r = lax.fori_loop(0, n_tiles // group, sources, jnp.zeros((256, 256), F32), unroll=True)
     for i in range(4):
         t = jnp.concatenate([r[0:128, i * 64 : i * 64 + 64], r[128:256, i * 64 : i * 64 + 64]], axis=1)
         if i == 0:

time: 76.4 us -> 75.8 us (level)
  waiting for transfers between devices: 9.97 us -> 11 us
  Pallas kernels: 21.6 us -> 20.6 us
  transfers between devices with their start and end apart: 9 -> 9, of which waited for: 4 -> 5; matrix products, arithmetic and copies ran while one was open for 2% -> 2% of each run, Pallas kernels for 23% -> 22%
where the time goes in v4:
time: 75.8 us; the launch traced here: 75.5 us
  starting transfers between devices  21 us (28%)
  Pallas kernels  20.6 us (27%)
  blocking collectives  18.4 us (24%)
  waiting for transfers between devices  11 us (15%)
  local copies, waits for them, and re-layouts  3.38 us (4%)
  between operations  0.8 us (1%)
    all_to_all x1, blocking collectives, on_device(): back = lax.all_to_all(back, 'tile', 0, 0, tiled=True)  18.4 us
    all_to_all x1, starting transfers between devices, on_device(): recv = lax.all_to_all(sent, 'tile', 0, 0, tiled=True)  8.17 us
    pallas_call x1, Pallas kernels, on_device(): pl.pallas_call(functools.partial(pair_kernel, scale), in_specs=[VM, VM],...  7.13 us
    ppermute x2, waiting for transfers between devices, on_device(): lax.ppermute(parts, 'mem', [(m, m ^ step) for m in range(n_groups)])  5.56 us
    pallas_call x1, Pallas kernels, on_device(): pl.pallas_call(pack_kernel, in_specs=[SM] + [HBM] * 5, out_specs=[VM] * 3...  5.11 us
    ppermute x1, starting transfers between devices, on_device(): lax.ppermute(parts, 'mem', [(m, n_groups - 1 - m) for m in range(n_groups)])  4.69 us
    all_to_all x1, waiting for transfers between devices, on_device(): recv = lax.all_to_all(sent, 'tile', 0, 0, tiled=True)  2.93 us
    pallas_call x1, Pallas kernels, on_device(): pl.pallas_call(image_kernel, in_specs=[VM] * 7, out_specs=VM, out_shape=s...  2.89 us
  transfers between devices with their start and end apart: 9, of which 5 were waited for; matrix products, arithmetic and copies ran while one was open for 2% of the time, Pallas kernels for 22%

profile of v4, /device:TPU:1, one launch (start us, length us, event | category | flops | bytes accessed | tf_op | source)
XLA Modules:
  0.0 75.5 jit_solution(13854928839884635474)
XLA Ops:
  0.6 1.0 %constant_dynamic-slice_fusion = bf16[10,2,16,512]{3,2,1,0:T(8,128)(2,1)S(1)} fusion(bf16[10,4,16,512]{3,2,1,0:T(8,128)(2,1)} %members_any.1, s32[]{:T(128)S(6)} %select_n.11), kind=kLoop, calls=%fused_computation.2 | loop fusion | bytes 655364 | tf_op jit(solution)/shard_map/swap/dynamic_slice | solution.py:476
  1.7 2.6 %collective-permute-start = (bf16[10,2,16,512]{3,2,1,0:T(8,128)(2,1)S(1)}, bf16[10,2,16,512]{3,2,1,0:T(8,128)(2,1)S(1)}, u32[]{:S(2)}, u32[]{:S(2)}) collective-permute-start(bf16[10,2,16,512]{3,2,1,0:T(8,128)(2,1)S(1)} %constant_dynamic-slice_fusion), channel_id=1, source_target_pairs={{0,1},{1,0},{2,3},{3,2},{4,5},{5,4},{6,7},{7,6},{8,9},{9,8},{10,11... | collective-permute-start | bytes 983048 | tf_op jit(solution)/shard_map/swap/ppermute | solution.py:477
  4.2 5.1 %pack.1 = (bf16[32,80,128]{2,1,0:T(8,128)(2,1)}, bf16[128,2048]{1,0:T(8,128)(2,1)}, bf16[10,2,16,512]{3,2,1,0:T(8,128)(2,1)}) custom-call(s32[1]{0:T(128)} %bitcast.half_ref, bf16[2048,128]{1,0:T(8,128)(2,1)} %w_any.1, f32[4,2048]{1,0:T(4,128)} %modes_any.1, s32[1,2048]{1,0:T(1,128)} %bitcast.3, s32[1,2048]{1,0:T(1,128)} %bitcast.5, ...), custom_call_target="tpu_custom_call" | custom-call | tf_op jit(solution)/shard_map/pack/pallas_call | solution.py:479
  9.3 0.0 copy-start.2
  9.3 8.2 %all-to-all-start = ((bf16[32,80,128]{2,1,0:T(8,128)(2,1)}), bf16[32,80,128]{2,1,0:T(8,128)(2,1)S(1)}, u32[]{:S(2)}, u32[]{:S(2)}) async-start(bf16[32,80,128]{2,1,0:T(8,128)(2,1)} %get-tuple-element.11), calls=%async_computation | async-start | bytes 1310720 | tf_op jit(solution)/shard_map/forward/all_to_all | solution.py:502
  17.5 1.1 %fusion = (bf16[10,2,4,512]{3,2,1,0:T(4,128)(2,1)S(1)}, bf16[10,2,4,512]{3,2,1,0:T(4,128)(2,1)S(1)}) fusion(bf16[10,2,16,512]{3,2,1,0:T(8,128)(2,1)} %get-tuple-element.12.keep_ref), kind=kLoop, calls=%fused_computation.3 | loop fusion | bytes 327680 | tf_op jit(solution)/shard_map/member_edges/slice | solution.py:508
  18.6 0.0 collective-permute-done.got_ref
  18.6 0.1 fusion.1
  18.7 0.1 pad_maximum_fusion
  18.8 1.7 %collective-permute-start.3 = (bf16[20,2,4,512]{3,2,1,0:T(4,128)(2,1)S(1)}, bf16[20,2,4,512]{3,2,1,0:T(4,128)(2,1)S(1)}, u32[]{:S(2)}, u32[]{:S(2)}) collective-permute-start(bf16[20,2,4,512]{3,2,1,0:T(4,128)(2,1)S(1)} %pad_maximum_fusion), channel_id=1, source_target_pairs={{0,8},{8,16},{16,24},{24,32},{32,40},{40,48},{48,56},{56,64},{64,7... | collective-permute-start | bytes 491528 | tf_op jit(solution)/shard_map/member_edges/ppermute | solution.py:511
  20.5 0.1 pad_maximum_fusion.1
  20.6 0.1 collective-permute-start.4
  20.7 0.0 copy-done.2
  20.7 7.1 %pairs.1 = (f32[25,8,16,128]{3,2,1,0:T(8,128)}, f32[16,8,16,128]{3,2,1,0:T(8,128)}, bf16[20,4,16,128]{3,2,1,0:T(8,128)(2,1)S(1)}) custom-call(bf16[10,2,16,512]{3,2,1,0:T(8,128)(2,1)S(1)} %copy-done.2, bf16[10,2,16,512]{3,2,1,0:T(8,128)(2,1)S(1)} %collective-permute-done.got_ref), custom_call_target="tpu_custom_call" | custom-call | bytes 29520000 | tf_op jit(solution)/shard_map/pairs/pallas_call | solution.py:515
  27.8 0.0 copy-start
  27.9 2.9 %all-to-all-done.recv_ref = bf16[32,80,128]{2,1,0:T(8,128)(2,1)S(1)} async-done(((bf16[32,80,128]{2,1,0:T(8,128)(2,1)}), bf16[32,80,128]{2,1,0:T(8,128)(2,1)S(1)}, u32[]{:S(2)}, u32[]{:S(2)}) %all-to-all-start) | async-done | bytes 655392 | tf_op jit(solution)/shard_map/forward/all_to_all | solution.py:502
  30.8 1.7 %spread.1 = (f32[32,16,128]{2,1,0:T(8,128)S(1)}, f32[128,128]{1,0:T(8,128)S(1)}, f32[128,128]{1,0:T(8,128)S(1)}) custom-call(bf16[32,80,128]{2,1,0:T(8,128)(2,1)S(1)} %all-to-all-done.recv_ref, bf16[20,4,16,128]{3,2,1,0:T(8,128)(2,1)S(1)} %get-tuple-element.13.after_ref.ends_ref), custom_call_target="tpu_custom_call" | custom-call | tf_op jit(solution)/shard_map/spread/pallas_call | solution.py:536
  32.5 0.1 collective-permute-start.1
  32.6 0.8 %collective-permute-start.2 = (f32[128,128]{1,0:T(8,128)S(1)}, f32[128,128]{1,0:T(8,128)S(1)}, u32[]{:S(2)}, u32[]{:S(2)}) collective-permute-start(f32[128,128]{1,0:T(8,128)S(1)} %get-tuple-element.16.after_ref), channel_id=1, source_target_pairs={{8,0},{16,8},{24,16},{32,24},{40,32},{48,40},{56,48},{64,56},{72,6... | collective-permute-start | bytes 196616 | tf_op jit(solution)/shard_map/spread_edges/ppermute | solution.py:553
  33.4 0.0 collective-permute-done.3.low_ref
  33.4 0.0 collective-permute-done.4.high_ref
  33.4 2.4 %pair_edges.1.ce_ref = f32[16,8,8,128]{3,2,1,0:T(8,128)S(1)} custom-call(bf16[20,4,16,128]{3,2,1,0:T(8,128)(2,1)S(1)} %get-tuple-element.13.after_ref.ends_ref, bf16[20,2,4,512]{3,2,1,0:T(4,128)(2,1)S(1)} %collective-permute-done.3.low_ref, bf16[20,2,4,512]{3,2,1,0:T(4,128)(2,1)S(1)} %collective-permute-done.4.high_ref, ...), custom_call_target="tpu_custom_call" | custom-call | bytes 11070000 | tf_op jit(solution)/shard_map/pair_edges/pallas_call | solution.py:555
  35.8 0.0 collective-permute-done.1.low_ref
  35.9 0.5 collective-permute-done.2.high_ref
  36.4 0.0 copy-done
  36.4 0.0 copy-start.1
  36.4 1.2 %copy-done.1 = f32[16,8,16,128]{3,2,1,0:T(8,128)S(1)} copy-done((f32[16,8,16,128]{3,2,1,0:T(8,128)S(1)}, f32[16,8,16,128]{3,2,1,0:T(8,128)}, u32[]{:S(2)}) %copy-start.1) | copy-done | bytes 1048600
  37.6 0.0 copy-start.3
  37.6 0.0 copy-start.4
  37.6 2.9 %images.1 = f32[17,8,128]{2,1,0:T(8,128)S(1)} custom-call(bf16[32,80,128]{2,1,0:T(8,128)(2,1)S(1)} %all-to-all-done.recv_ref, f32[32,16,128]{2,1,0:T(8,128)S(1)} %get-tuple-element.14.f_ref, f32[128,128]{1,0:T(8,128)S(1)} %collective-permute-done.1.low_ref, f32[128,128]{1,0:T(8,128)S(1)} %collective-permute-done.2.high_ref, f32[25,8,16,128]{3,2,1,0:T(8,128)S(1)} %copy-done, ...), custom_call_target="tpu_custom_call" | custom-call | tf_op jit(solution)/shard_map/images/pallas_call | solution.py:569
  40.5 0.1 collective-permute-start.5
  40.6 3.1 %collective-permute-done.5 = f32[17,8,128]{2,1,0:T(8,128)S(1)} collective-permute-done((f32[17,8,128]{2,1,0:T(8,128)S(1)}, f32[17,8,128]{2,1,0:T(8,128)S(1)}, u32[]{:S(2)}, u32[]{:S(2)}) %collective-permute-start.5) | collective-permute-done | bytes 69664 | tf_op jit(solution)/shard_map/group_sum/ppermute | solution.py:584
  43.7 2.8 %collective-permute-start.6 = (f32[17,8,128]{2,1,0:T(8,128)S(1)}, f32[17,8,128]{2,1,0:T(8,128)S(1)}, u32[]{:S(2)}, u32[]{:S(2)}) collective-permute-start(f32[17,8,128]{2,1,0:T(8,128)S(1)} %add.16), channel_id=1, source_target_pairs={{0,3},{1,2},{2,1},{3,0},{4,7},{5,6},{6,5},{7,4},{8,11},{9,10},{10,... | collective-permute-start | bytes 208904 | tf_op jit(solution)/shard_map/group_sum/ppermute | solution.py:584
  46.5 2.4 %collective-permute-done.6 = f32[17,8,128]{2,1,0:T(8,128)S(1)} collective-permute-done((f32[17,8,128]{2,1,0:T(8,128)S(1)}, f32[17,8,128]{2,1,0:T(8,128)S(1)}, u32[]{:S(2)}, u32[]{:S(2)}) %collective-permute-start.6) | collective-permute-done | bytes 69664 | tf_op jit(solution)/shard_map/group_sum/ppermute | solution.py:584
  49.0 4.7 %collective-permute-start.7 = (f32[17,8,128]{2,1,0:T(8,128)S(1)}, f32[17,8,128]{2,1,0:T(8,128)S(1)}, u32[]{:S(2)}, u32[]{:S(2)}) collective-permute-start(f32[17,8,128]{2,1,0:T(8,128)S(1)} %add.17.parts_ref), channel_id=1, source_target_pairs={{0,7},{1,6},{2,5},{3,4},{4,3},{5,2},{6,1},{7,0},{8,15},{9,14},{10,... | collective-permute-start | bytes 208904 | tf_op jit(solution)/shard_map/group_sum/ppermute | solution.py:585
  53.7 2.0 %collective-permute-done.7.other_ref = f32[17,8,128]{2,1,0:T(8,128)S(1)} collective-permute-done((f32[17,8,128]{2,1,0:T(8,128)S(1)}, f32[17,8,128]{2,1,0:T(8,128)S(1)}, u32[]{:S(2)}, u32[]{:S(2)}) %collective-permute-start.7) | collective-permute-done | bytes 69664 | tf_op jit(solution)/shard_map/group_sum/ppermute | solution.py:585
  55.7 0.1 gram.1
  55.8 18.4 %all_to_all.10.back_ref = f32[32,8,128]{2,1,0:T(8,128)S(1)} all-to-all(f32[32,8,128]{2,1,0:T(8,128)S(1)} %gram.1), channel_id=1, replica_groups=mesh['tile'=32,'mem'=8] {'tile'}, dimensions={0} | all-to-all | bytes 262144 | tf_op jit(solution)/shard_map/return/all_to_all | solution.py:595
  74.2 0.0 copy-done.3
  74.2 0.0 copy-done.4
  74.2 1.3 %finish.1 = (f32[4,2048]{1,0:T(4,128)}, f32[4]{0:T(128)}) custom-call(f32[32,8,128]{2,1,0:T(8,128)S(1)} %all_to_all.10.back_ref, bf16[128,2048]{1,0:T(8,128)(2,1)S(1)} %copy-done.3, s32[1,2048]{1,0:T(1,128)S(1)} %bitcast.4), custom_call_target="tpu_custom_call" | custom-call | tf_op jit(solution)/shard_map/finish/pallas_call | solution.py:597
  (2 shorter events, 0.0 us)
Async XLA Ops:
  1.7 16.9 %collective-permute-start = (bf16[10,2,16,512]{3,2,1,0:T(8,128)(2,1)S(1)}, bf16[10,2,16,512]{3,2,1,0:T(8,128)(2,1)S(1)}, u32[]{:S(2)}, u32[]{:S(2)}) collective-permute-start(bf16[10,2,16,512]{3,2,1,0:T(8,128)(2,1)S(1)} %constant_dynamic-slice_fusion), channel_id=1, source_target_pairs={{0,1},{1,0},{2,3},{3,2},{4,5},{5,4},{6,7},{7,6},{8,9},{9,8},{10,11... | collective-permute-start | bytes 983048 | tf_op jit(solution)/shard_map/swap/ppermute | solution.py:477
  9.3 11.4 %copy-start.2 = (bf16[10,2,16,512]{3,2,1,0:T(8,128)(2,1)S(1)}, bf16[10,2,16,512]{3,2,1,0:T(8,128)(2,1)}, u32[]{:S(2)}) copy-start(bf16[10,2,16,512]{3,2,1,0:T(8,128)(2,1)} %get-tuple-element.12.keep_ref) | copy-start | bytes 983044
  9.3 21.5 %all-to-all-start = ((bf16[32,80,128]{2,1,0:T(8,128)(2,1)}), bf16[32,80,128]{2,1,0:T(8,128)(2,1)S(1)}, u32[]{:S(2)}, u32[]{:S(2)}) async-start(bf16[32,80,128]{2,1,0:T(8,128)(2,1)} %get-tuple-element.11), calls=%async_computation | async-start | bytes 1310720 | tf_op jit(solution)/shard_map/forward/all_to_all | solution.py:502
  18.8 14.6 %collective-permute-start.3 = (bf16[20,2,4,512]{3,2,1,0:T(4,128)(2,1)S(1)}, bf16[20,2,4,512]{3,2,1,0:T(4,128)(2,1)S(1)}, u32[]{:S(2)}, u32[]{:S(2)}) collective-permute-start(bf16[20,2,4,512]{3,2,1,0:T(4,128)(2,1)S(1)} %pad_maximum_fusion), channel_id=1, source_target_pairs={{0,8},{8,16},{16,24},{24,32},{32,40},{40,48},{48,56},{56,64},{64,7... | collective-permute-start | bytes 491528 | tf_op jit(solution)/shard_map/member_edges/ppermute | solution.py:511
  20.6 12.8 %collective-permute-start.4 = (bf16[20,2,4,512]{3,2,1,0:T(4,128)(2,1)S(1)}, bf16[20,2,4,512]{3,2,1,0:T(4,128)(2,1)S(1)}, u32[]{:S(2)}, u32[]{:S(2)}) collective-permute-start(bf16[20,2,4,512]{3,2,1,0:T(4,128)(2,1)S(1)} %pad_maximum_fusion.1), channel_id=1, source_target_pairs={{8,0},{16,8},{24,16},{32,24},{40,32},{48,40},{56,48},{64,56},{72,6... | collective-permute-start | bytes 491528 | tf_op jit(solution)/shard_map/member_edges/ppermute | solution.py:512
  27.8 8.5 %copy-start = (f32[25,8,16,128]{3,2,1,0:T(8,128)S(1)}, f32[25,8,16,128]{3,2,1,0:T(8,128)}, u32[]{:S(2)}) copy-start(f32[25,8,16,128]{3,2,1,0:T(8,128)} %get-tuple-element.17.behind_ref) | copy-start | bytes 4915204
  32.5 3.3 %collective-permute-start.1 = (f32[128,128]{1,0:T(8,128)S(1)}, f32[128,128]{1,0:T(8,128)S(1)}, u32[]{:S(2)}, u32[]{:S(2)}) collective-permute-start(f32[128,128]{1,0:T(8,128)S(1)} %get-tuple-element.15), channel_id=1, source_target_pairs={{0,8},{8,16},{16,24},{24,32},{32,40},{40,48},{48,56},{56,64},{64,7... | collective-permute-start | bytes 196616 | tf_op jit(solution)/shard_map/spread_edges/ppermute | solution.py:552
  32.6 3.8 %collective-permute-start.2 = (f32[128,128]{1,0:T(8,128)S(1)}, f32[128,128]{1,0:T(8,128)S(1)}, u32[]{:S(2)}, u32[]{:S(2)}) collective-permute-start(f32[128,128]{1,0:T(8,128)S(1)} %get-tuple-element.16.after_ref), channel_id=1, source_target_pairs={{8,0},{16,8},{24,16},{32,24},{40,32},{48,40},{56,48},{64,56},{72,6... | collective-permute-start | bytes 196616 | tf_op jit(solution)/shard_map/spread_edges/ppermute | solution.py:553
  36.4 1.2 %copy-start.1 = (f32[16,8,16,128]{3,2,1,0:T(8,128)S(1)}, f32[16,8,16,128]{3,2,1,0:T(8,128)}, u32[]{:S(2)}) copy-start(f32[16,8,16,128]{3,2,1,0:T(8,128)} %get-tuple-element.18.ahead_ref) | copy-start | bytes 3145732
  37.6 36.6 %copy-start.3 = (bf16[128,2048]{1,0:T(8,128)(2,1)S(1)}, bf16[128,2048]{1,0:T(8,128)(2,1)}, u32[]{:S(2)}) copy-start(bf16[128,2048]{1,0:T(8,128)(2,1)} %get-tuple-element.19.hot_ref) | copy-start | bytes 1572868
  37.6 36.6 %copy-start.4 = (s32[2048,1]{0,1:T(1,128)S(1)}, s32[2048,1]{0,1:T(1,128)}, u32[]{:S(2)}) copy-start(s32[2048,1]{0,1:T(1,128)} %param.8) | copy-start | bytes 24580
  40.5 3.2 %collective-permute-start.5 = (f32[17,8,128]{2,1,0:T(8,128)S(1)}, f32[17,8,128]{2,1,0:T(8,128)S(1)}, u32[]{:S(2)}, u32[]{:S(2)}) collective-permute-start(f32[17,8,128]{2,1,0:T(8,128)S(1)} %images.1), channel_id=1, source_target_pairs={{0,1},{1,0},{2,3},{3,2},{4,5},{5,4},{6,7},{7,6},{8,9},{9,8},{10,11... | collective-permute-start | bytes 208904 | tf_op jit(solution)/shard_map/group_sum/ppermute | solution.py:584
  43.7 5.2 %collective-permute-start.6 = (f32[17,8,128]{2,1,0:T(8,128)S(1)}, f32[17,8,128]{2,1,0:T(8,128)S(1)}, u32[]{:S(2)}, u32[]{:S(2)}) collective-permute-start(f32[17,8,128]{2,1,0:T(8,128)S(1)} %add.16), channel_id=1, source_target_pairs={{0,3},{1,2},{2,1},{3,0},{4,7},{5,6},{6,5},{7,4},{8,11},{9,10},{10,... | collective-permute-start | bytes 208904 | tf_op jit(solution)/shard_map/group_sum/ppermute | solution.py:584
  49.0 6.7 %collective-permute-start.7 = (f32[17,8,128]{2,1,0:T(8,128)S(1)}, f32[17,8,128]{2,1,0:T(8,128)S(1)}, u32[]{:S(2)}, u32[]{:S(2)}) collective-permute-start(f32[17,8,128]{2,1,0:T(8,128)S(1)} %add.17.parts_ref), channel_id=1, source_target_pairs={{0,7},{1,6},{2,5},{3,4},{4,3},{5,2},{6,1},{7,0},{8,15},{9,14},{10,... | collective-permute-start | bytes 208904 | tf_op jit(solution)/shard_map/group_sum/ppermute | solution.py:585

commit v5 on v4

--- a/solution.py
+++ b/solution.py
@@ -363,7 +363,7 @@
         return cross, square
 
     zero = jnp.zeros((MODES, 128), F32)
-    cross, square = lax.fori_loop(0, n_tiles // group, image, (zero, zero), unroll=2)
+    cross, square = lax.fori_loop(0, n_tiles // group, image, (zero, zero), unroll=True)
     out_ref[n_tiles // 2, 0:4, :] = cross
     out_ref[n_tiles // 2, 4:8, :] = square
 

time: 75.8 us -> 75.5 us (level)
  no operation moved by 1% of the time
where the time goes in v5:
time: 75.5 us; the launch traced here: 75.2 us
  starting transfers between devices  21 us (28%)
  Pallas kernels  20.4 us (27%)
  blocking collectives  18.4 us (24%)
  waiting for transfers between devices  11 us (15%)
  local copies, waits for them, and re-layouts  3.38 us (4%)
  between operations  0.79 us (1%)
    all_to_all x1, blocking collectives, on_device(): back = lax.all_to_all(back, 'tile', 0, 0, tiled=True)  18.4 us
    all_to_all x1, starting transfers between devices, on_device(): recv = lax.all_to_all(sent, 'tile', 0, 0, tiled=True)  8.17 us
    pallas_call x1, Pallas kernels, on_device(): pl.pallas_call(functools.partial(pair_kernel, scale), in_specs=[VM, VM],...  7.13 us
    ppermute x2, waiting for transfers between devices, on_device(): lax.ppermute(parts, 'mem', [(m, m ^ step) for m in range(n_groups)])  5.55 us
    pallas_call x1, Pallas kernels, on_device(): pl.pallas_call(pack_kernel, in_specs=[SM] + [HBM] * 5, out_specs=[VM] * 3...  5.11 us
    ppermute x1, starting transfers between devices, on_device(): lax.ppermute(parts, 'mem', [(m, n_groups - 1 - m) for m in range(n_groups)])  4.7 us
    all_to_all x1, waiting for transfers between devices, on_device(): recv = lax.all_to_all(sent, 'tile', 0, 0, tiled=True)  2.93 us
    ppermute x2, starting transfers between devices, on_device(): lax.ppermute(parts, 'mem', [(m, m ^ step) for m in range(n_groups)])  2.89 us
  transfers between devices with their start and end apart: 9, of which 5 were waited for; matrix products, arithmetic and copies ran while one was open for 2% of the time, Pallas kernels for 22%

profile of v5, /device:TPU:1, one launch (start us, length us, event | category | flops | bytes accessed | tf_op | source)
XLA Modules:
  0.0 75.2 jit_solution(16200459600800831055)
XLA Ops:
  0.6 1.0 %constant_dynamic-slice_fusion = bf16[10,2,16,512]{3,2,1,0:T(8,128)(2,1)S(1)} fusion(bf16[10,4,16,512]{3,2,1,0:T(8,128)(2,1)} %members_any.1, s32[]{:T(128)S(6)} %select_n.11), kind=kLoop, calls=%fused_computation.2 | loop fusion | bytes 655364 | tf_op jit(solution)/shard_map/swap/dynamic_slice | solution.py:476
  1.7 2.6 %collective-permute-start = (bf16[10,2,16,512]{3,2,1,0:T(8,128)(2,1)S(1)}, bf16[10,2,16,512]{3,2,1,0:T(8,128)(2,1)S(1)}, u32[]{:S(2)}, u32[]{:S(2)}) collective-permute-start(bf16[10,2,16,512]{3,2,1,0:T(8,128)(2,1)S(1)} %constant_dynamic-slice_fusion), channel_id=1, source_target_pairs={{0,1},{1,0},{2,3},{3,2},{4,5},{5,4},{6,7},{7,6},{8,9},{9,8},{10,11... | collective-permute-start | bytes 983048 | tf_op jit(solution)/shard_map/swap/ppermute | solution.py:477
  4.2 5.1 %pack.1 = (bf16[32,80,128]{2,1,0:T(8,128)(2,1)}, bf16[128,2048]{1,0:T(8,128)(2,1)}, bf16[10,2,16,512]{3,2,1,0:T(8,128)(2,1)}) custom-call(s32[1]{0:T(128)} %bitcast.half_ref, bf16[2048,128]{1,0:T(8,128)(2,1)} %w_any.1, f32[4,2048]{1,0:T(4,128)} %modes_any.1, s32[1,2048]{1,0:T(1,128)} %bitcast.3, s32[1,2048]{1,0:T(1,128)} %bitcast.5, ...), custom_call_target="tpu_custom_call" | custom-call | tf_op jit(solution)/shard_map/pack/pallas_call | solution.py:479
  9.3 0.0 copy-start.2
  9.3 8.2 %all-to-all-start = ((bf16[32,80,128]{2,1,0:T(8,128)(2,1)}), bf16[32,80,128]{2,1,0:T(8,128)(2,1)S(1)}, u32[]{:S(2)}, u32[]{:S(2)}) async-start(bf16[32,80,128]{2,1,0:T(8,128)(2,1)} %get-tuple-element.11), calls=%async_computation | async-start | bytes 1310720 | tf_op jit(solution)/shard_map/forward/all_to_all | solution.py:502
  17.5 1.1 %fusion = (bf16[10,2,4,512]{3,2,1,0:T(4,128)(2,1)S(1)}, bf16[10,2,4,512]{3,2,1,0:T(4,128)(2,1)S(1)}) fusion(bf16[10,2,16,512]{3,2,1,0:T(8,128)(2,1)} %get-tuple-element.12.keep_ref), kind=kLoop, calls=%fused_computation.3 | loop fusion | bytes 327680 | tf_op jit(solution)/shard_map/member_edges/slice | solution.py:508
  18.6 0.0 collective-permute-done.got_ref
  18.6 0.1 fusion.1
  18.7 0.1 pad_maximum_fusion
  18.8 1.7 %collective-permute-start.3 = (bf16[20,2,4,512]{3,2,1,0:T(4,128)(2,1)S(1)}, bf16[20,2,4,512]{3,2,1,0:T(4,128)(2,1)S(1)}, u32[]{:S(2)}, u32[]{:S(2)}) collective-permute-start(bf16[20,2,4,512]{3,2,1,0:T(4,128)(2,1)S(1)} %pad_maximum_fusion), channel_id=1, source_target_pairs={{0,8},{8,16},{16,24},{24,32},{32,40},{40,48},{48,56},{56,64},{64,7... | collective-permute-start | bytes 491528 | tf_op jit(solution)/shard_map/member_edges/ppermute | solution.py:511
  20.5 0.1 pad_maximum_fusion.1
  20.6 0.1 collective-permute-start.4
  20.7 0.0 copy-done.2
  20.7 7.1 %pairs.1 = (f32[25,8,16,128]{3,2,1,0:T(8,128)}, f32[16,8,16,128]{3,2,1,0:T(8,128)}, bf16[20,4,16,128]{3,2,1,0:T(8,128)(2,1)S(1)}) custom-call(bf16[10,2,16,512]{3,2,1,0:T(8,128)(2,1)S(1)} %copy-done.2, bf16[10,2,16,512]{3,2,1,0:T(8,128)(2,1)S(1)} %collective-permute-done.got_ref), custom_call_target="tpu_custom_call" | custom-call | bytes 29520000 | tf_op jit(solution)/shard_map/pairs/pallas_call | solution.py:515
  27.8 0.0 copy-start
  27.9 2.9 %all-to-all-done.recv_ref = bf16[32,80,128]{2,1,0:T(8,128)(2,1)S(1)} async-done(((bf16[32,80,128]{2,1,0:T(8,128)(2,1)}), bf16[32,80,128]{2,1,0:T(8,128)(2,1)S(1)}, u32[]{:S(2)}, u32[]{:S(2)}) %all-to-all-start) | async-done | bytes 655392 | tf_op jit(solution)/shard_map/forward/all_to_all | solution.py:502
  30.8 1.7 %spread.1 = (f32[32,16,128]{2,1,0:T(8,128)S(1)}, f32[128,128]{1,0:T(8,128)S(1)}, f32[128,128]{1,0:T(8,128)S(1)}) custom-call(bf16[32,80,128]{2,1,0:T(8,128)(2,1)S(1)} %all-to-all-done.recv_ref, bf16[20,4,16,128]{3,2,1,0:T(8,128)(2,1)S(1)} %get-tuple-element.13.after_ref.ends_ref), custom_call_target="tpu_custom_call" | custom-call | tf_op jit(solution)/shard_map/spread/pallas_call | solution.py:536
  32.5 0.1 collective-permute-start.1
  32.6 0.8 %collective-permute-start.2 = (f32[128,128]{1,0:T(8,128)S(1)}, f32[128,128]{1,0:T(8,128)S(1)}, u32[]{:S(2)}, u32[]{:S(2)}) collective-permute-start(f32[128,128]{1,0:T(8,128)S(1)} %get-tuple-element.16.after_ref), channel_id=1, source_target_pairs={{8,0},{16,8},{24,16},{32,24},{40,32},{48,40},{56,48},{64,56},{72,6... | collective-permute-start | bytes 196616 | tf_op jit(solution)/shard_map/spread_edges/ppermute | solution.py:553
  33.4 0.0 collective-permute-done.3.low_ref
  33.4 0.0 collective-permute-done.4.high_ref
  33.4 2.4 %pair_edges.1.ce_ref = f32[16,8,8,128]{3,2,1,0:T(8,128)S(1)} custom-call(bf16[20,4,16,128]{3,2,1,0:T(8,128)(2,1)S(1)} %get-tuple-element.13.after_ref.ends_ref, bf16[20,2,4,512]{3,2,1,0:T(4,128)(2,1)S(1)} %collective-permute-done.3.low_ref, bf16[20,2,4,512]{3,2,1,0:T(4,128)(2,1)S(1)} %collective-permute-done.4.high_ref, ...), custom_call_target="tpu_custom_call" | custom-call | bytes 11070000 | tf_op jit(solution)/shard_map/pair_edges/pallas_call | solution.py:555
  35.8 0.0 collective-permute-done.1.low_ref
  35.9 0.5 collective-permute-done.2.high_ref
  36.4 0.0 copy-done
  36.4 0.0 copy-start.1
  36.4 1.2 %copy-done.1 = f32[16,8,16,128]{3,2,1,0:T(8,128)S(1)} copy-done((f32[16,8,16,128]{3,2,1,0:T(8,128)S(1)}, f32[16,8,16,128]{3,2,1,0:T(8,128)}, u32[]{:S(2)}) %copy-start.1) | copy-done | bytes 1048600
  37.6 0.0 copy-start.3
  37.6 0.0 copy-start.4
  37.6 2.6 %images.1 = f32[17,8,128]{2,1,0:T(8,128)S(1)} custom-call(bf16[32,80,128]{2,1,0:T(8,128)(2,1)S(1)} %all-to-all-done.recv_ref, f32[32,16,128]{2,1,0:T(8,128)S(1)} %get-tuple-element.14.f_ref, f32[128,128]{1,0:T(8,128)S(1)} %collective-permute-done.1.low_ref, f32[128,128]{1,0:T(8,128)S(1)} %collective-permute-done.2.high_ref, f32[25,8,16,128]{3,2,1,0:T(8,128)S(1)} %copy-done, ...), custom_call_target="tpu_custom_call" | custom-call | tf_op jit(solution)/shard_map/images/pallas_call | solution.py:569
  40.2 0.1 collective-permute-start.5
  40.3 3.1 %collective-permute-done.5 = f32[17,8,128]{2,1,0:T(8,128)S(1)} collective-permute-done((f32[17,8,128]{2,1,0:T(8,128)S(1)}, f32[17,8,128]{2,1,0:T(8,128)S(1)}, u32[]{:S(2)}, u32[]{:S(2)}) %collective-permute-start.5) | collective-permute-done | bytes 69664 | tf_op jit(solution)/shard_map/group_sum/ppermute | solution.py:584
  43.5 2.8 %collective-permute-start.6 = (f32[17,8,128]{2,1,0:T(8,128)S(1)}, f32[17,8,128]{2,1,0:T(8,128)S(1)}, u32[]{:S(2)}, u32[]{:S(2)}) collective-permute-start(f32[17,8,128]{2,1,0:T(8,128)S(1)} %add.16), channel_id=1, source_target_pairs={{0,3},{1,2},{2,1},{3,0},{4,7},{5,6},{6,5},{7,4},{8,11},{9,10},{10,... | collective-permute-start | bytes 208904 | tf_op jit(solution)/shard_map/group_sum/ppermute | solution.py:584
  46.3 2.4 %collective-permute-done.6 = f32[17,8,128]{2,1,0:T(8,128)S(1)} collective-permute-done((f32[17,8,128]{2,1,0:T(8,128)S(1)}, f32[17,8,128]{2,1,0:T(8,128)S(1)}, u32[]{:S(2)}, u32[]{:S(2)}) %collective-permute-start.6) | collective-permute-done | bytes 69664 | tf_op jit(solution)/shard_map/group_sum/ppermute | solution.py:584
  48.7 4.7 %collective-permute-start.7 = (f32[17,8,128]{2,1,0:T(8,128)S(1)}, f32[17,8,128]{2,1,0:T(8,128)S(1)}, u32[]{:S(2)}, u32[]{:S(2)}) collective-permute-start(f32[17,8,128]{2,1,0:T(8,128)S(1)} %add.17.parts_ref), channel_id=1, source_target_pairs={{0,7},{1,6},{2,5},{3,4},{4,3},{5,2},{6,1},{7,0},{8,15},{9,14},{10,... | collective-permute-start | bytes 208904 | tf_op jit(solution)/shard_map/group_sum/ppermute | solution.py:585
  53.4 2.0 %collective-permute-done.7.other_ref = f32[17,8,128]{2,1,0:T(8,128)S(1)} collective-permute-done((f32[17,8,128]{2,1,0:T(8,128)S(1)}, f32[17,8,128]{2,1,0:T(8,128)S(1)}, u32[]{:S(2)}, u32[]{:S(2)}) %collective-permute-start.7) | collective-permute-done | bytes 69664 | tf_op jit(solution)/shard_map/group_sum/ppermute | solution.py:585
  55.4 0.1 gram.1
  55.5 18.4 %all_to_all.10.back_ref = f32[32,8,128]{2,1,0:T(8,128)S(1)} all-to-all(f32[32,8,128]{2,1,0:T(8,128)S(1)} %gram.1), channel_id=1, replica_groups=mesh['tile'=32,'mem'=8] {'tile'}, dimensions={0} | all-to-all | bytes 262144 | tf_op jit(solution)/shard_map/return/all_to_all | solution.py:595
  73.9 0.0 copy-done.3
  73.9 0.0 copy-done.4
  73.9 1.3 %finish.1 = (f32[4,2048]{1,0:T(4,128)}, f32[4]{0:T(128)}) custom-call(f32[32,8,128]{2,1,0:T(8,128)S(1)} %all_to_all.10.back_ref, bf16[128,2048]{1,0:T(8,128)(2,1)S(1)} %copy-done.3, s32[1,2048]{1,0:T(1,128)S(1)} %bitcast.4), custom_call_target="tpu_custom_call" | custom-call | tf_op jit(solution)/shard_map/finish/pallas_call | solution.py:597
  (2 shorter events, 0.0 us)
Async XLA Ops:
  1.7 16.9 %collective-permute-start = (bf16[10,2,16,512]{3,2,1,0:T(8,128)(2,1)S(1)}, bf16[10,2,16,512]{3,2,1,0:T(8,128)(2,1)S(1)}, u32[]{:S(2)}, u32[]{:S(2)}) collective-permute-start(bf16[10,2,16,512]{3,2,1,0:T(8,128)(2,1)S(1)} %constant_dynamic-slice_fusion), channel_id=1, source_target_pairs={{0,1},{1,0},{2,3},{3,2},{4,5},{5,4},{6,7},{7,6},{8,9},{9,8},{10,11... | collective-permute-start | bytes 983048 | tf_op jit(solution)/shard_map/swap/ppermute | solution.py:477
  9.3 11.4 %copy-start.2 = (bf16[10,2,16,512]{3,2,1,0:T(8,128)(2,1)S(1)}, bf16[10,2,16,512]{3,2,1,0:T(8,128)(2,1)}, u32[]{:S(2)}) copy-start(bf16[10,2,16,512]{3,2,1,0:T(8,128)(2,1)} %get-tuple-element.12.keep_ref) | copy-start | bytes 983044
  9.3 21.5 %all-to-all-start = ((bf16[32,80,128]{2,1,0:T(8,128)(2,1)}), bf16[32,80,128]{2,1,0:T(8,128)(2,1)S(1)}, u32[]{:S(2)}, u32[]{:S(2)}) async-start(bf16[32,80,128]{2,1,0:T(8,128)(2,1)} %get-tuple-element.11), calls=%async_computation | async-start | bytes 1310720 | tf_op jit(solution)/shard_map/forward/all_to_all | solution.py:502
  18.8 14.6 %collective-permute-start.3 = (bf16[20,2,4,512]{3,2,1,0:T(4,128)(2,1)S(1)}, bf16[20,2,4,512]{3,2,1,0:T(4,128)(2,1)S(1)}, u32[]{:S(2)}, u32[]{:S(2)}) collective-permute-start(bf16[20,2,4,512]{3,2,1,0:T(4,128)(2,1)S(1)} %pad_maximum_fusion), channel_id=1, source_target_pairs={{0,8},{8,16},{16,24},{24,32},{32,40},{40,48},{48,56},{56,64},{64,7... | collective-permute-start | bytes 491528 | tf_op jit(solution)/shard_map/member_edges/ppermute | solution.py:511
  20.6 12.8 %collective-permute-start.4 = (bf16[20,2,4,512]{3,2,1,0:T(4,128)(2,1)S(1)}, bf16[20,2,4,512]{3,2,1,0:T(4,128)(2,1)S(1)}, u32[]{:S(2)}, u32[]{:S(2)}) collective-permute-start(bf16[20,2,4,512]{3,2,1,0:T(4,128)(2,1)S(1)} %pad_maximum_fusion.1), channel_id=1, source_target_pairs={{8,0},{16,8},{24,16},{32,24},{40,32},{48,40},{56,48},{64,56},{72,6... | collective-permute-start | bytes 491528 | tf_op jit(solution)/shard_map/member_edges/ppermute | solution.py:512
  27.8 8.5 %copy-start = (f32[25,8,16,128]{3,2,1,0:T(8,128)S(1)}, f32[25,8,16,128]{3,2,1,0:T(8,128)}, u32[]{:S(2)}) copy-start(f32[25,8,16,128]{3,2,1,0:T(8,128)} %get-tuple-element.17.behind_ref) | copy-start | bytes 4915204
  32.5 3.3 %collective-permute-start.1 = (f32[128,128]{1,0:T(8,128)S(1)}, f32[128,128]{1,0:T(8,128)S(1)}, u32[]{:S(2)}, u32[]{:S(2)}) collective-permute-start(f32[128,128]{1,0:T(8,128)S(1)} %get-tuple-element.15), channel_id=1, source_target_pairs={{0,8},{8,16},{16,24},{24,32},{32,40},{40,48},{48,56},{56,64},{64,7... | collective-permute-start | bytes 196616 | tf_op jit(solution)/shard_map/spread_edges/ppermute | solution.py:552
  32.6 3.8 %collective-permute-start.2 = (f32[128,128]{1,0:T(8,128)S(1)}, f32[128,128]{1,0:T(8,128)S(1)}, u32[]{:S(2)}, u32[]{:S(2)}) collective-permute-start(f32[128,128]{1,0:T(8,128)S(1)} %get-tuple-element.16.after_ref), channel_id=1, source_target_pairs={{8,0},{16,8},{24,16},{32,24},{40,32},{48,40},{56,48},{64,56},{72,6... | collective-permute-start | bytes 196616 | tf_op jit(solution)/shard_map/spread_edges/ppermute | solution.py:553
  36.4 1.2 %copy-start.1 = (f32[16,8,16,128]{3,2,1,0:T(8,128)S(1)}, f32[16,8,16,128]{3,2,1,0:T(8,128)}, u32[]{:S(2)}) copy-start(f32[16,8,16,128]{3,2,1,0:T(8,128)} %get-tuple-element.18.ahead_ref) | copy-start | bytes 3145732
  37.6 36.3 %copy-start.3 = (bf16[128,2048]{1,0:T(8,128)(2,1)S(1)}, bf16[128,2048]{1,0:T(8,128)(2,1)}, u32[]{:S(2)}) copy-start(bf16[128,2048]{1,0:T(8,128)(2,1)} %get-tuple-element.19.hot_ref) | copy-start | bytes 1572868
  37.6 36.4 %copy-start.4 = (s32[2048,1]{0,1:T(1,128)S(1)}, s32[2048,1]{0,1:T(1,128)}, u32[]{:S(2)}) copy-start(s32[2048,1]{0,1:T(1,128)} %param.8) | copy-start | bytes 24580
  40.2 3.2 %collective-permute-start.5 = (f32[17,8,128]{2,1,0:T(8,128)S(1)}, f32[17,8,128]{2,1,0:T(8,128)S(1)}, u32[]{:S(2)}, u32[]{:S(2)}) collective-permute-start(f32[17,8,128]{2,1,0:T(8,128)S(1)} %images.1), channel_id=1, source_target_pairs={{0,1},{1,0},{2,3},{3,2},{4,5},{5,4},{6,7},{7,6},{8,9},{9,8},{10,11... | collective-permute-start | bytes 208904 | tf_op jit(solution)/shard_map/group_sum/ppermute | solution.py:584
  43.5 5.2 %collective-permute-start.6 = (f32[17,8,128]{2,1,0:T(8,128)S(1)}, f32[17,8,128]{2,1,0:T(8,128)S(1)}, u32[]{:S(2)}, u32[]{:S(2)}) collective-permute-start(f32[17,8,128]{2,1,0:T(8,128)S(1)} %add.16), channel_id=1, source_target_pairs={{0,3},{1,2},{2,1},{3,0},{4,7},{5,6},{6,5},{7,4},{8,11},{9,10},{10,... | collective-permute-start | bytes 208904 | tf_op jit(solution)/shard_map/group_sum/ppermute | solution.py:584
  48.7 6.7 %collective-permute-start.7 = (f32[17,8,128]{2,1,0:T(8,128)S(1)}, f32[17,8,128]{2,1,0:T(8,128)S(1)}, u32[]{:S(2)}, u32[]{:S(2)}) collective-permute-start(f32[17,8,128]{2,1,0:T(8,128)S(1)} %add.17.parts_ref), channel_id=1, source_target_pairs={{0,7},{1,6},{2,5},{3,4},{4,3},{5,2},{6,1},{7,0},{8,15},{9,14},{10,... | collective-permute-start | bytes 208904 | tf_op jit(solution)/shard_map/group_sum/ppermute | solution.py:585
